TPU v7x, 512 devices: a whole 4x4x16 slice. The times are simulated.
512 devices in a mesh: det: 64 (over x, z), tm: 8 (over y, core).
Axes of the slice: x: 4, y: 4, z: 16, core: 2. Of those that a mesh axis runs over, the one named last changes fastest.
Arguments:
- timestream: bfloat16 [8192, 1024], P('det', 'tm'), may hold values from -6 to 6
- pointing: int32 [8192, 1024], P('det', 'tm'), may hold values from 0 to 65535
- detector_band: int32 [8192], P('det'), may hold values from 0 to 19
- mode_loading: bfloat16 [8192, 64], P('det'), may hold values from -0.29492188 to 0.29492188
- mode_mix: float32 [20, 64, 64], replicated, may hold values from -0.36 to 0.36
- noise_weight: float32 [8192], P('det'), may hold values from 0.3 to 3
- ownership: int32 [512], replicated, may hold values from 0 to 511, each once
Outputs:
- amplitudes: float32 [1280, 1024], P(None, 'tm')
- sky_map: float32 [512, 128], P('det')
Inputs may be any that keep to these rules, and one draw needn't show every extreme that they name: `ownership`: each tile appears once.
All inputs are finite; a program needn't handle non-finite values.
Results may differ from a plain program's by a relative error of at most 0.0037.
Values sent between devices are 32-bit elements; how exact they have to be, the bound alone decides.
No kernel may reach another device: no remote copies, remote signals or barrier semaphores. Data moves between devices by JAX's collectives and lax.ppermute only.
A program may use at most 64 MiB of HBM per device.

v0:
```python
import functools

import jax
import jax.numpy as jnp
from jax import lax
from jax.experimental import pallas as pl
from jax.experimental.pallas import tpu as pltpu
from jax.sharding import Mesh, PartitionSpec as P

TILE_PIX = 128
HALF = 256
GROUP = 8
EXTRA = 8
F32 = jnp.float32
BF16 = jnp.bfloat16


def lanes(rows, width):
    return lax.broadcasted_iota(jnp.int32, (rows, 128), 1) // width


def turn(x, amount):
    amount %= 128
    return pltpu.roll(x, amount, 1) if amount else x


def split(x):
    high = x.astype(BF16)
    low = (x - high.astype(F32)).astype(BF16)
    return high, low


def pack_kernel(nx, *refs):
    sources, (out_ref, *held, sems) = refs[:5], refs[5:]
    copies = [
        pltpu.make_async_copy(src, dst, sems.at[n]) for n, (src, dst) in enumerate(zip(sources, held))
    ]
    for copy in copies:
        copy.start()
    for copy in copies:
        copy.wait()
    loading_t_ref, band_ref, noise_ref, ts_ref, point_ref = held
    modes, dets = loading_t_ref.shape
    width = ts_ref.shape[1] // nx
    rows = dets + EXTRA
    ts = ts_ref[...].astype(F32)
    point = point_ref[...].astype(F32)
    loading_t = loading_t_ref[...].astype(F32)
    loading = jnp.concatenate([jnp.zeros((128 - modes, dets), F32), loading_t], axis=0).T
    group = lanes(dets, width)
    for d in range(nx):
        body = jnp.where(group == 0, turn(ts, -width * d), turn(point, width - width * d))
        out_ref[d * rows:d * rows + dets, :] = jnp.where(group < 2, body, loading)
        out_ref[d * rows + dets:(d + 1) * rows, :] = jnp.concatenate(
            [band_ref[...].astype(F32), noise_ref[...], jnp.zeros((EXTRA - 2, dets), F32)], axis=0
        )


def project_kernel(ns, owners, bands, modes, got_ref, out_ref):
    rows = got_ref.shape[0] // ns
    dets = rows - EXTRA
    width = 128 // ns
    per = modes * width // 128
    quad = per // owners
    pair = 8 // quad
    group = lanes(dets, width)
    slot = (lax.broadcasted_iota(jnp.int32, (bands * quad, dets), 0) // quad).astype(F32)
    left, right = [], []
    for s in range(ns):
        chunk = got_ref[s * rows:s * rows + dets, :]
        loading_t = chunk.T[128 - modes:, :]
        ts = jnp.where(group == 0, chunk, 0.0)
        pick = jnp.where(slot == got_ref[s * rows + dets:s * rows + dets + 1, :], 1.0, 0.0)
        pick = pick.reshape(bands // pair, 8, dets)
        for j in range(modes // per):
            parts = [loading_t[j * per + o * quad:j * per + (o + 1) * quad, :] for o in range(owners)]
            part = jnp.stack([jnp.concatenate([p] * pair, axis=0) for p in parts])
            wide = (part[:, None] * pick[None]).reshape(owners * bands * quad, dets)
            left.append(wide.astype(BF16))
            right.append(turn(ts, width * j).astype(BF16))
    out_ref[...] = jnp.dot(
        jnp.concatenate(left, axis=1), jnp.concatenate(right, axis=0), preferred_element_type=F32
    )


def row(ref, i, times):
    return jnp.broadcast_to(ref[pl.ds(i, 1), :], (16, times)).astype(BF16)[None]


def add_bins(value_ref, hi_ref, lo_ref, acc_ref):
    dets, times = value_ref.shape
    ids = lax.broadcasted_iota(jnp.int32, (HALF, times), 0).astype(F32).astype(BF16)
    ids = ids.reshape(HALF // 16, 16, times)
    one = jnp.ones((), BF16)
    zero = jnp.zeros((), BF16)

    def body(g, carry):
        left, right = [], []
        for k in range(GROUP):
            i = g * GROUP + k
            upper = row(hi_ref, i, times) == ids
            lower = row(lo_ref, i, times) == ids
            left.append(jnp.where(upper, one, zero).reshape(HALF, times))
            right.append(jnp.where(lower, row(value_ref, i, times), zero).reshape(HALF, times))
        added = lax.dot_general(
            jnp.concatenate(left, axis=1),
            jnp.concatenate(right, axis=1),
            (((1,), (1,)), ((), ())),
            preferred_element_type=F32,
        )
        acc_ref[:HALF, :] += added[:, :TILE_PIX]
        acc_ref[HALF:, :] += added[:, TILE_PIX:]
        return carry

    lax.fori_loop(0, dets // GROUP, body, 0, unroll=4)


def sum_kernel(count, parts_ref, out_ref):
    rows = parts_ref.shape[0] // count
    total = parts_ref[:rows, :]
    for s in range(1, count):
        total = total + parts_ref[s * rows:(s + 1) * rows, :]
    for s in range(out_ref.shape[0] // rows):
        out_ref[s * rows:(s + 1) * rows, :] = total


def weighted_kernel(
    nx, bands, modes, got_ref, own_ref, wide_ref, noise_ref, hi_ref, lo_ref, acc_ref, place_ref, value_s
):
    tiles = place_ref.shape[0]
    own = own_ref[...]
    own = jnp.broadcast_to(((own & 1) * HALF + (own >> 1)).astype(F32), (128, tiles))
    step = min(128, tiles)
    source = lax.broadcasted_iota(jnp.int32, (step, 2 * HALF), 1).astype(F32)
    for r in range(0, tiles, step):
        here = own[:, r:r + step].T[:, 0:1]
        place_ref[r:r + step, :] = jnp.where(
            jnp.broadcast_to(here, (step, 2 * HALF)) == source, 1.0, 0.0
        ).astype(BF16)
    rows = got_ref.shape[0] // nx
    dets = rows - EXTRA
    width = 128 // nx
    group = lanes(dets, width)
    half = lanes(dets, modes)
    for s in range(nx):
        chunk = got_ref[s * rows:s * rows + dets, :]
        tail = got_ref[s * rows + dets:(s + 1) * rows, :]
        columns = jnp.concatenate([tail, jnp.zeros((128 - EXTRA, dets), F32)], axis=0).T
        band_off = jnp.broadcast_to(columns[:, 0:1], (dets, 128)) - half.astype(F32)
        loading2 = jnp.where(half == 0, turn(chunk, modes), chunk)
        for b in range(0, bands, 2):
            wide_ref[s * dets:(s + 1) * dets, b * modes:(b + 2) * modes] = jnp.where(
                band_off == float(b), loading2, 0.0
            ).astype(BF16)
        here = (
            jnp.broadcast_to(columns[:, 1:2], (dets, 128)),
            turn(chunk, width * s),
            turn(chunk, width * (s - 1)),
        )
        total = here if s == 0 else tuple(
            jnp.where(group == s, a, b) for a, b in zip(here, total)
        )
    noise, ts, point = total
    noise_ref[...] = noise
    value_s[...] = (noise * ts).astype(BF16).astype(F32)
    point = point.astype(jnp.int32)
    hi_ref[...] = (point >> 8).astype(F32)
    lo_ref[...] = (point & 255).astype(F32)
    acc_ref[...] = jnp.zeros_like(acc_ref)
    add_bins(value_s, hi_ref, lo_ref, acc_ref)


def correct_kernel(
    nx, owners, bands, proj_ref, mix_ref, wide_ref, noise_ref, hi_ref, lo_ref, start_ref, place_ref,
    amp_ref, map_ref, value_s, acc_s
):
    modes = mix_ref.shape[1]
    dets = noise_ref.shape[0]
    width = 128 // nx
    per = modes // nx
    quad = per // owners
    group = lanes(per, width)
    rounded = []
    for b in range(bands):
        starts = [(o * bands + b) * quad for o in range(owners)]
        mine = jnp.concatenate([proj_ref[at:at + quad, :] for at in starts], axis=0)
        turned = [turn(mine, width * k) for k in range(nx)]
        pieces = []
        for j in range(nx):
            piece = turned[(0 - j) % nx]
            for g in range(1, nx):
                piece = jnp.where(group == g, turned[(g - j) % nx], piece)
            pieces.append(piece)
        p = jnp.concatenate(pieces, axis=0)
        mh, ml = split(mix_ref[b])
        ph, plow = split(p)
        amp = p + jnp.dot(
            jnp.concatenate([mh, ml, mh], axis=1),
            jnp.concatenate([ph, ph, plow], axis=0),
            preferred_element_type=F32,
        )
        rounded.append(amp.astype(BF16))
        packed = amp[:per, :]
        for j in range(1, nx):
            packed = jnp.where(group == j, amp[j * per:(j + 1) * per, :], packed)
        amp_ref[b * per:(b + 1) * per, :] = packed
    fits = jnp.dot(wide_ref[...], jnp.concatenate(rounded, axis=0), preferred_element_type=F32)
    group = lanes(dets, width)
    fitted = fits[:dets, :]
    for s in range(1, nx):
        fitted = jnp.where(group == s, fits[s * dets:(s + 1) * dets, :], fitted)
    value_s[...] = -(noise_ref[...] * fitted).astype(BF16).astype(F32)
    acc_s[...] = start_ref[...]
    add_bins(value_s, hi_ref, lo_ref, acc_s)
    high, low = split(acc_s[...])
    placed = jnp.dot(place_ref[...], jnp.concatenate([high, low], axis=1), preferred_element_type=F32)
    map_ref[...] = placed[:, :TILE_PIX] + placed[:, TILE_PIX:]


def gather_kernel(nx, bands, *refs):
    parts, out_ref = refs[:nx], refs[nx]
    per = parts[0].shape[0] // bands
    width = 128 // nx
    group = lanes(per, width)
    mine = lax.axis_index("x")
    sources = [lax.rem(mine + nx - k, nx) for k in range(nx)]
    for b in range(bands):
        for j in range(nx):
            total = jnp.zeros((per, 128), F32)
            for k in range(nx):
                piece = parts[k][b * per:(b + 1) * per, :]
                moved = pltpu.roll(piece, lax.rem(sources[k] + nx - j, nx) * width, 1)
                total = jnp.where(group == sources[k], moved, total)
            out_ref[(b * nx + j) * per:(b * nx + j + 1) * per, :] = total


def add_over(x, axes):
    swapped = lax.all_to_all(x, axes, 0, 0, tiled=True)
    return swapped.reshape((lax.axis_size(axes), -1) + x.shape[1:]).sum(0)


def copy_over(x, axes):
    count = lax.axis_size(axes)
    spread = jnp.broadcast_to(x[None], (count,) + x.shape).reshape((-1,) + x.shape[1:])
    return lax.all_to_all(spread, axes, 0, 0, tiled=True)


def per_device(
    timestream, pointing, detector_band, mode_loading, mode_mix, noise_weight, ownership
):
    dets, times = timestream.shape
    bands, modes = mode_mix.shape[:2]
    tiles = ownership.shape[0]
    nx, nh, nl = lax.axis_size("x"), lax.axis_size("zh"), lax.axis_size("zl")
    nt = lax.axis_size("y") * lax.axis_size("core")
    vmem = pl.BlockSpec(memory_space=pltpu.VMEM)
    params = pltpu.CompilerParams(vmem_limit_bytes=32 * 1024 * 1024)

    bin_cost = pl.CostEstimate(
        flops=2 * dets * times * HALF * HALF, bytes_accessed=1 << 21, transcendentals=0
    )

    def call(kernel, shapes, args, specs=None, scratch=(), cost=None, limit=params, types=None):
        return pl.pallas_call(
            kernel,
            out_shape=tuple(
                jax.ShapeDtypeStruct(s, t) for s, t in zip(shapes, types or [F32] * len(shapes))
            ),
            in_specs=specs or [vmem] * len(args),
            out_specs=tuple(vmem for _ in shapes),
            scratch_shapes=scratch,
            compiler_params=limit,
            cost_estimate=cost,
        )(*args)

    inputs = (mode_loading.T, detector_band[None, :], noise_weight[None, :], timestream, pointing)
    (packed,) = call(
        functools.partial(pack_kernel, nx),
        [(nx * (dets + EXTRA), 128)],
        inputs,
        specs=[pl.BlockSpec(memory_space=pltpu.HBM)] * 5,
        scratch=[pltpu.VMEM(a.shape, a.dtype) for a in inputs] + [pltpu.SemaphoreType.DMA((5,))],
        limit=None,
    )
    got = lax.all_to_all(packed, "x", 0, 0, tiled=True)
    (local,) = call(
        functools.partial(project_kernel, nx, nl, bands, modes),
        [(bands * modes // nx, 128)],
        (got,),
    )
    swapped = lax.all_to_all(local, "zl", 0, 0, tiled=True)
    (copies,) = call(
        functools.partial(sum_kernel, nl), [(nh * local.shape[0] // nl, 128)], (swapped,)
    )
    copies, got = lax.optimization_barrier((copies, got))
    wide, noise, hi, lo, start, place = call(
        functools.partial(weighted_kernel, nx, bands, modes),
        [(nx * dets, bands * modes)] + [(dets, times)] * 3 + [(2 * HALF, TILE_PIX), (tiles, 2 * HALF)],
        (got, ownership[None, :]),
        scratch=[pltpu.VMEM((dets, times), F32)],
        cost=bin_cost,
        types=[BF16] + [F32] * 4 + [BF16],
    )
    share = add_over(copies, "zh")
    share, wide, noise, hi, lo, start, place = lax.optimization_barrier(
        (share, wide, noise, hi, lo, start, place)
    )
    projected = copy_over(share, "zl")
    amp, part = call(
        functools.partial(correct_kernel, nx, nl, bands),
        [(bands * modes // nx, 128), (tiles, TILE_PIX)],
        (projected, mode_mix, wide, noise, hi, lo, start, place),
        scratch=[pltpu.VMEM((dets, times), F32), pltpu.VMEM((2 * HALF, TILE_PIX), F32)],
        cost=bin_cost,
    )
    moved = [
        lax.ppermute(amp, "x", [(i, (i + k) % nx) for i in range(nx)]) for k in range(1, nx)
    ]
    share = add_over(part, ("x", "zh", "zl"))
    share, *moved = lax.optimization_barrier((share, *moved))
    sky_map = copy_over(share, ("y", "core")).reshape((nt,) + share.shape).sum(0)
    (amplitudes,) = call(
        functools.partial(gather_kernel, nx, bands), [(bands * modes, times)], (amp, *moved)
    )
    return amplitudes, sky_map


def solution(mesh):
    fine = Mesh(mesh.devices.reshape(4, 4, 4, 4, 2), ("x", "zh", "zl", "y", "core"))
    det, tm = ("x", "zh", "zl"), ("y", "core")
    placed = (P(det, tm), P(det, tm), P(det), P(det, None), P(), P(det), P())
    return jax.shard_map(
        per_device,
        mesh=fine,
        in_specs=placed,
        out_specs=(P(None, tm), P(det, None)),
        check_vma=False,
    )
```

profile of v0, /device:TPU:1, one launch (start us, length us, event | category | flops | bytes accessed | tf_op | source)
XLA Modules:
  0.0 102.3 jit_solution(782371946924389062)
XLA Ops:
  0.6 0.0 copy-start.1
  0.6 1.8 %shard_map.86 = f32[544,128]{1,0:T(8,128)} custom-call(bf16[64,128]{1,0:T(8,128)(2,1)} %bitcast.18, s32[1,128]{1,0:T(1,128)} %bitcast.19, f32[1,128]{1,0:T(1,128)} %bitcast.20, bf16[128,128]{1,0:T(8,128)(2,1)} %refs_3_.1, s32[128,128]{1,0:T(8,128)} %refs_4_.1), custom_call_target="tpu_custom_call" | custom-call | tf_op jit(solution)/shard_map/pallas_call | solution.py:264
  2.5 10.5 %all_to_all.54 = f32[4,136,128]{2,1,0:T(8,128)S(1)} all-to-all(f32[4,136,128]{2,1,0:T(8,128)} %bitcast.17), channel_id=1, replica_groups=mesh['x'=4,'zh'=4,'zl'=4,'y'=4,'core'=2] {'x'}, dimensions={0} | all-to-all | bytes 557056 | tf_op jit(solution)/shard_map/all_to_all | solution.py:285
  13.0 0.6 shard_map.87
  13.6 11.0 %all_to_all.55 = f32[4,80,128]{2,1,0:T(8,128)S(1)} all-to-all(f32[4,80,128]{2,1,0:T(8,128)S(1)} %bitcast.13), channel_id=1, replica_groups=mesh['x'=4,'zh'=4,'zl'=4,'y'=4,'core'=2] {'zl'}, dimensions={0} | all-to-all | bytes 327680 | tf_op jit(solution)/shard_map/all_to_all | solution.py:291
  24.6 0.7 shard_map.88
  25.3 12.1 %all-to-all-start.2 = ((f32[4,80,128]{2,1,0:T(8,128)}), f32[4,80,128]{2,1,0:T(8,128)S(1)}, u32[]{:S(2)}, u32[]{:S(2)}) async-start(f32[4,80,128]{2,1,0:T(8,128)} %bitcast.7), calls=%async_computation.2 | async-start | bytes 327680 | tf_op jit(solution)/shard_map/all_to_all | solution.py:238
  37.4 0.0 copy-done.1
  37.4 0.0 copy-start
  37.4 3.8 %shard_map.89 = (bf16[512,1280]{1,0:T(8,128)(2,1)S(1)}, f32[128,128]{1,0:T(8,128)S(1)}, f32[128,128]{1,0:T(8,128)S(1)}, f32[128,128]{1,0:T(8,128)S(1)}, f32[512,...) custom-call(f32[544,128]{1,0:T(8,128)S(1)} %bitcast.12, s32[1,512]{1,0:T(1,128)S(1)} %bitcast.16), custom_call_target="tpu_custom_call" | custom-call | flops 2147483648 | bytes 2097152 | tf_op jit(solution)/shard_map/pallas_call | solution.py:264
  41.1 8.5 %all-to-all-done.2 = f32[4,80,128]{2,1,0:T(8,128)S(1)} async-done(((f32[4,80,128]{2,1,0:T(8,128)}), f32[4,80,128]{2,1,0:T(8,128)S(1)}, u32[]{:S(2)}, u32[]{:S(2)}) %all-to-all-start.2) | async-done | bytes 163872 | tf_op jit(solution)/shard_map/all_to_all | solution.py:238
  49.7 8.4 %all_to_all.56 = f32[4,80,128]{2,1,0:T(8,128)S(1)} all-to-all(f32[4,80,128]{2,1,0:T(8,128)S(1)} %broadcast_in_dim.24), channel_id=1, replica_groups=mesh['x'=4,'zh'=4,'zl'=4,'y'=4,'core'=2] {'zl'}, dimensions={0} | all-to-all | bytes 327680 | tf_op jit(solution)/shard_map/all_to_all | solution.py:245
  58.0 0.0 copy-done
  58.0 4.9 %shard_map.90 = (f32[320,128]{1,0:T(8,128)S(1)}, f32[512,128]{1,0:T(8,128)}) custom-call(f32[320,128]{1,0:T(8,128)S(1)} %bitcast.15, f32[20,64,64]{2,1,0:T(8,128)S(1)} %copy-done, bf16[512,1280]{1,0:T(8,128)(2,1)S(1)} %get-tuple-element.32.wide_ref, f32[128,128]{1,0:T(8,128)S(1)} %get-tuple-element.33.noise_ref, f32[128,128]{1,0:T(8,128)S(1)} %get-tuple-element.34.hi_ref, ...), custom_call_target="tpu_custom_call" | custom-call | flops 2147483648 | bytes 2097152 | tf_op jit(solution)/shard_map/pallas_call | solution.py:264
  62.9 6.1 %all-to-all-start.4 = ((f32[64,8,128]{2,1,0:T(8,128)}), f32[64,8,128]{2,1,0:T(8,128)S(1)}, u32[]{:S(2)}, u32[]{:S(2)}) async-start(f32[64,8,128]{2,1,0:T(8,128)} %bitcast.10), calls=%async_computation.4 | async-start | bytes 524288 | tf_op jit(solution)/shard_map/all_to_all | solution.py:238
  69.1 4.3 %collective-permute-start.2 = (f32[320,128]{1,0:T(8,128)S(1)}, f32[320,128]{1,0:T(8,128)S(1)}, u32[]{:S(2)}, u32[]{:S(2)}) collective-permute-start(f32[320,128]{1,0:T(8,128)S(1)} %get-tuple-element.38.refs_0_), channel_id=1, source_target_pairs={{0,384},{128,0},{256,128},{384,256},{1,385},{129,1},{257,129},{385... | collective-permute-start | bytes 491528 | tf_op jit(solution)/shard_map/ppermute | solution.py:317
  73.4 2.3 %collective-permute-start.1 = (f32[320,128]{1,0:T(8,128)S(1)}, f32[320,128]{1,0:T(8,128)S(1)}, u32[]{:S(2)}, u32[]{:S(2)}) collective-permute-start(f32[320,128]{1,0:T(8,128)S(1)} %get-tuple-element.38.refs_0_), channel_id=1, source_target_pairs={{0,256},{128,384},{256,0},{384,128},{1,257},{129,385},{257,1},{385... | collective-permute-start | bytes 491528 | tf_op jit(solution)/shard_map/ppermute | solution.py:317
  75.7 2.6 %collective-permute-start = (f32[320,128]{1,0:T(8,128)S(1)}, f32[320,128]{1,0:T(8,128)S(1)}, u32[]{:S(2)}, u32[]{:S(2)}) collective-permute-start(f32[320,128]{1,0:T(8,128)S(1)} %get-tuple-element.38.refs_0_), channel_id=1, source_target_pairs={{0,128},{128,256},{256,384},{384,0},{1,129},{129,257},{257,385},{3... | collective-permute-start | bytes 491528 | tf_op jit(solution)/shard_map/ppermute | solution.py:317
  78.3 6.3 %all-to-all-done.4 = f32[64,8,128]{2,1,0:T(8,128)S(1)} async-done(((f32[64,8,128]{2,1,0:T(8,128)}), f32[64,8,128]{2,1,0:T(8,128)S(1)}, u32[]{:S(2)}, u32[]{:S(2)}) %all-to-all-start.4) | async-done | bytes 262176 | tf_op jit(solution)/shard_map/all_to_all | solution.py:238
  84.6 0.1 reduce_sum.28
  84.6 0.0 collective-permute-done.2.refs_3_
  84.6 0.0 collective-permute-done.1.refs_2_
  84.7 0.0 collective-permute-done.refs_1_
  84.7 0.6 broadcast_in_dim.25
  85.3 11.7 %all-to-all-start.5 = ((f32[8,8,128]{2,1,0:T(8,128)}), f32[8,8,128]{2,1,0:T(8,128)S(1)}, u32[]{:S(2)}, u32[]{:S(2)}) async-start(f32[8,8,128]{2,1,0:T(8,128)} %broadcast_in_dim.25), calls=%async_computation.5 | async-start | bytes 65536 | tf_op jit(solution)/shard_map/all_to_all | solution.py:245
  97.0 1.6 %shard_map.91 = f32[1280,128]{1,0:T(8,128)} custom-call(f32[320,128]{1,0:T(8,128)S(1)} %get-tuple-element.38.refs_0_, f32[320,128]{1,0:T(8,128)S(1)} %collective-permute-done.refs_1_, f32[320,128]{1,0:T(8,128)S(1)} %collective-permute-done.1.refs_2_, f32[320,128]{1,0:T(8,128)S(1)} %collective-permute-done.2.refs_3_), custom_call_target="tpu_custom_call" | custom-call | tf_op jit(solution)/shard_map/pallas_call | solution.py:264
  98.6 3.1 %all-to-all-done.5 = f32[8,8,128]{2,1,0:T(8,128)S(1)} async-done(((f32[8,8,128]{2,1,0:T(8,128)}), f32[8,8,128]{2,1,0:T(8,128)S(1)}, u32[]{:S(2)}, u32[]{:S(2)}) %all-to-all-start.5) | async-done | bytes 32800 | tf_op jit(solution)/shard_map/all_to_all | solution.py:245
  101.7 0.6 reduce_sum.29
  (2 shorter events, 0.0 us)
Async XLA Ops:
  0.6 36.7 %copy-start.1 = (s32[512]{0:T(512)S(1)}, s32[512]{0:T(512)}, u32[]{:S(2)}) copy-start(s32[512]{0:T(512)} %param.13) | copy-start | bytes 6148
  25.3 24.4 %all-to-all-start.2 = ((f32[4,80,128]{2,1,0:T(8,128)}), f32[4,80,128]{2,1,0:T(8,128)S(1)}, u32[]{:S(2)}, u32[]{:S(2)}) async-start(f32[4,80,128]{2,1,0:T(8,128)} %bitcast.7), calls=%async_computation.2 | async-start | bytes 327680 | tf_op jit(solution)/shard_map/all_to_all | solution.py:238
  37.4 20.7 %copy-start = (f32[20,64,64]{2,1,0:T(8,128)S(1)}, f32[20,64,64]{2,1,0:T(8,128)}, u32[]{:S(2)}) copy-start(f32[20,64,64]{2,1,0:T(8,128)} %mix_ref.1) | copy-start | bytes 983044
  62.9 21.6 %all-to-all-start.4 = ((f32[64,8,128]{2,1,0:T(8,128)}), f32[64,8,128]{2,1,0:T(8,128)S(1)}, u32[]{:S(2)}, u32[]{:S(2)}) async-start(f32[64,8,128]{2,1,0:T(8,128)} %bitcast.10), calls=%async_computation.4 | async-start | bytes 524288 | tf_op jit(solution)/shard_map/all_to_all | solution.py:238
  69.1 15.6 %collective-permute-start.2 = (f32[320,128]{1,0:T(8,128)S(1)}, f32[320,128]{1,0:T(8,128)S(1)}, u32[]{:S(2)}, u32[]{:S(2)}) collective-permute-start(f32[320,128]{1,0:T(8,128)S(1)} %get-tuple-element.38.refs_0_), channel_id=1, source_target_pairs={{0,384},{128,0},{256,128},{384,256},{1,385},{129,1},{257,129},{385... | collective-permute-start | bytes 491528 | tf_op jit(solution)/shard_map/ppermute | solution.py:317
  73.4 11.2 %collective-permute-start.1 = (f32[320,128]{1,0:T(8,128)S(1)}, f32[320,128]{1,0:T(8,128)S(1)}, u32[]{:S(2)}, u32[]{:S(2)}) collective-permute-start(f32[320,128]{1,0:T(8,128)S(1)} %get-tuple-element.38.refs_0_), channel_id=1, source_target_pairs={{0,256},{128,384},{256,0},{384,128},{1,257},{129,385},{257,1},{385... | collective-permute-start | bytes 491528 | tf_op jit(solution)/shard_map/ppermute | solution.py:317
  75.7 9.0 %collective-permute-start = (f32[320,128]{1,0:T(8,128)S(1)}, f32[320,128]{1,0:T(8,128)S(1)}, u32[]{:S(2)}, u32[]{:S(2)}) collective-permute-start(f32[320,128]{1,0:T(8,128)S(1)} %get-tuple-element.38.refs_0_), channel_id=1, source_target_pairs={{0,128},{128,256},{256,384},{384,0},{1,129},{129,257},{257,385},{3... | collective-permute-start | bytes 491528 | tf_op jit(solution)/shard_map/ppermute | solution.py:317
  85.3 16.4 %all-to-all-start.5 = ((f32[8,8,128]{2,1,0:T(8,128)}), f32[8,8,128]{2,1,0:T(8,128)S(1)}, u32[]{:S(2)}, u32[]{:S(2)}) async-start(f32[8,8,128]{2,1,0:T(8,128)} %broadcast_in_dim.25), calls=%async_computation.5 | async-start | bytes 65536 | tf_op jit(solution)/shard_map/all_to_all | solution.py:245
where the time goes:
time: 103 us; the launch traced here: 102 us
  starting transfers between devices  39.1 us (38%)
  blocking collectives  29.8 us (29%)
  waiting for transfers between devices  17.9 us (17%)
  Pallas kernels  13.4 us (13%)
    all_to_all x2, starting transfers between devices, add_over(): swapped = lax.all_to_all(x, axes, 0, 0, tiled=True)  18.2 us
    all_to_all x2, waiting for transfers between devices, add_over(): swapped = lax.all_to_all(x, axes, 0, 0, tiled=True)  14.8 us
    pallas_call x6, Pallas kernels, call(): pl.pallas_call(kernel, out_shape=tuple((jax.ShapeDtypeStruct(s, t) for s,...  13.4 us
    all_to_all x1, starting transfers between devices, copy_over(): return lax.all_to_all(spread, axes, 0, 0, tiled=True)  11.7 us
    all_to_all x1, blocking collectives, per_device(): swapped = lax.all_to_all(local, 'zl', 0, 0, tiled=True)  11 us
    all_to_all x1, blocking collectives, per_device(): got = lax.all_to_all(packed, 'x', 0, 0, tiled=True)  10.5 us
    ppermute x3, starting transfers between devices, per_device(): lax.ppermute(amp, 'x', [(i, (i + k) % nx) for i in range(nx)])  9.2 us
    all_to_all x1, blocking collectives, copy_over(): return lax.all_to_all(spread, axes, 0, 0, tiled=True)  8.37 us
  transfers between devices with their start and end apart: 6, of which 3 were waited for; matrix products, arithmetic and copies ran while one was open for 0% of the time, Pallas kernels for 5%

commit v1 on v0

--- a/solution.py
+++ b/solution.py
@@ -28,6 +28,11 @@
     high = x.astype(BF16)
     low = (x - high.astype(F32)).astype(BF16)
     return high, low
+
+
+def place_of(owner, owners, size):
+    turned = jnp.where(lax.axis_index("z") >= lax.axis_size("z") // 2, owners // 2, 0)
+    return pl.multiple_of(lax.rem(owner + turned, owners) * size, 8)
 
 
 def pack_kernel(nx, *refs):
@@ -78,9 +83,12 @@
             wide = (part[:, None] * pick[None]).reshape(owners * bands * quad, dets)
             left.append(wide.astype(BF16))
             right.append(turn(ts, width * j).astype(BF16))
-    out_ref[...] = jnp.dot(
+    total = jnp.dot(
         jnp.concatenate(left, axis=1), jnp.concatenate(right, axis=0), preferred_element_type=F32
     )
+    size = bands * quad
+    for o in range(owners):
+        out_ref[pl.ds(place_of(o, owners, size), size), :] = total[o * size:(o + 1) * size, :]
 
 
 def row(ref, i, times):
@@ -172,7 +180,7 @@
 
 def correct_kernel(
     nx, owners, bands, proj_ref, mix_ref, wide_ref, noise_ref, hi_ref, lo_ref, start_ref, place_ref,
-    amp_ref, map_ref, value_s, acc_s
+    amp_ref, map_ref, value_s, acc_s, shares_s
 ):
     modes = mix_ref.shape[1]
     dets = noise_ref.shape[0]
@@ -181,9 +189,12 @@
     quad = per // owners
     group = lanes(per, width)
     rounded = []
+    size = bands * quad
+    for o in range(owners):
+        shares_s[o * size:(o + 1) * size, :] = proj_ref[pl.ds(place_of(o, owners, size), size), :]
     for b in range(bands):
         starts = [(o * bands + b) * quad for o in range(owners)]
-        mine = jnp.concatenate([proj_ref[at:at + quad, :] for at in starts], axis=0)
+        mine = jnp.concatenate([shares_s[at:at + quad, :] for at in starts], axis=0)
         turned = [turn(mine, width * k) for k in range(nx)]
         pieces = []
         for j in range(nx):
@@ -234,15 +245,16 @@
             out_ref[(b * nx + j) * per:(b * nx + j + 1) * per, :] = total
 
 
-def add_over(x, axes):
-    swapped = lax.all_to_all(x, axes, 0, 0, tiled=True)
-    return swapped.reshape((lax.axis_size(axes), -1) + x.shape[1:]).sum(0)
-
-
-def copy_over(x, axes):
-    count = lax.axis_size(axes)
+def add_over(x, axes, groups=None):
+    swapped = lax.all_to_all(x, axes, 0, 0, tiled=True, axis_index_groups=groups)
+    count = len(groups[0]) if groups else lax.axis_size(axes)
+    return swapped.reshape((count, -1) + x.shape[1:]).sum(0)
+
+
+def copy_over(x, axes, groups=None):
+    count = len(groups[0]) if groups else lax.axis_size(axes)
     spread = jnp.broadcast_to(x[None], (count,) + x.shape).reshape((-1,) + x.shape[1:])
-    return lax.all_to_all(spread, axes, 0, 0, tiled=True)
+    return lax.all_to_all(spread, axes, 0, 0, tiled=True, axis_index_groups=groups)
 
 
 def per_device(
@@ -251,7 +263,13 @@
     dets, times = timestream.shape
     bands, modes = mode_mix.shape[:2]
     tiles = ownership.shape[0]
-    nx, nh, nl = lax.axis_size("x"), lax.axis_size("zh"), lax.axis_size("zl")
+    nx, nz = lax.axis_size("x"), lax.axis_size("z")
+    nl = 4
+    nh = nz // nl
+    quads = [[h * nl + p for p in range(nl)] for h in range(nh)]
+    rings = [
+        [h * nl + (o + (nl // 2 if h >= nh // 2 else 0)) % nl for h in range(nh)] for o in range(nl)
+    ]
     nt = lax.axis_size("y") * lax.axis_size("core")
     vmem = pl.BlockSpec(memory_space=pltpu.VMEM)
     params = pltpu.CompilerParams(vmem_limit_bytes=32 * 1024 * 1024)
@@ -288,7 +306,7 @@
         [(bands * modes // nx, 128)],
         (got,),
     )
-    swapped = lax.all_to_all(local, "zl", 0, 0, tiled=True)
+    swapped = lax.all_to_all(local, "z", 0, 0, tiled=True, axis_index_groups=quads)
     (copies,) = call(
         functools.partial(sum_kernel, nl), [(nh * local.shape[0] // nl, 128)], (swapped,)
     )
@@ -301,22 +319,26 @@
         cost=bin_cost,
         types=[BF16] + [F32] * 4 + [BF16],
     )
-    share = add_over(copies, "zh")
+    share = add_over(copies, "z", rings)
     share, wide, noise, hi, lo, start, place = lax.optimization_barrier(
         (share, wide, noise, hi, lo, start, place)
     )
-    projected = copy_over(share, "zl")
+    projected = copy_over(share, "z", quads)
     amp, part = call(
         functools.partial(correct_kernel, nx, nl, bands),
         [(bands * modes // nx, 128), (tiles, TILE_PIX)],
         (projected, mode_mix, wide, noise, hi, lo, start, place),
-        scratch=[pltpu.VMEM((dets, times), F32), pltpu.VMEM((2 * HALF, TILE_PIX), F32)],
+        scratch=[
+            pltpu.VMEM((dets, times), F32),
+            pltpu.VMEM((2 * HALF, TILE_PIX), F32),
+            pltpu.VMEM((bands * modes // nx, 128), F32),
+        ],
         cost=bin_cost,
     )
     moved = [
         lax.ppermute(amp, "x", [(i, (i + k) % nx) for i in range(nx)]) for k in range(1, nx)
     ]
-    share = add_over(part, ("x", "zh", "zl"))
+    share = add_over(part, ("x", "z"))
     share, *moved = lax.optimization_barrier((share, *moved))
     sky_map = copy_over(share, ("y", "core")).reshape((nt,) + share.shape).sum(0)
     (amplitudes,) = call(
@@ -326,8 +348,8 @@
 
 
 def solution(mesh):
-    fine = Mesh(mesh.devices.reshape(4, 4, 4, 4, 2), ("x", "zh", "zl", "y", "core"))
-    det, tm = ("x", "zh", "zl"), ("y", "core")
+    fine = Mesh(mesh.devices.reshape(4, 16, 4, 2), ("x", "z", "y", "core"))
+    det, tm = ("x", "z"), ("y", "core")
     placed = (P(det, tm), P(det, tm), P(det), P(det, None), P(), P(det), P())
     return jax.shard_map(
         per_device,

time: 103 us -> 101 us (0.981)
  starting transfers between devices: 39.1 us -> 36.5 us
  blocking collectives: 29.8 us -> 31.8 us
  waiting for transfers between devices: 17.9 us -> 16.1 us
    all_to_all x3, starting transfers between devices: 29.9 us -> 27.3 us  [the longest x2 15.5 us: add_over(): lax.all_to_all(x, axes, 0, 0, tiled=True, axis_index_groups=groups)]
    all_to_all x2, blocking collectives: 19.4 us -> 21.4 us  [the longest x1 11 us: per_device(): lax.all_to_all(local, 'z', 0, 0, tiled=True, axis_index_groups=quads)]
    all_to_all x3, waiting for transfers between devices: 17.9 us -> 16.1 us  [the longest x2 13 us: add_over(): lax.all_to_all(x, axes, 0, 0, tiled=True, axis_index_groups=groups)]
where the time goes in v1:
time: 101 us; the launch traced here: 100 us
  starting transfers between devices  36.5 us (36%)
  blocking collectives  31.8 us (31%)
  waiting for transfers between devices  16.1 us (16%)
  Pallas kernels  13.5 us (13%)
    all_to_all x2, starting transfers between devices, add_over(): lax.all_to_all(x, axes, 0, 0, tiled=True, axis_index_groups=groups)  15.5 us
    pallas_call x6, Pallas kernels, call(): pl.pallas_call(kernel, out_shape=tuple((jax.ShapeDtypeStruct(s, t) for s,...  13.5 us
    all_to_all x2, waiting for transfers between devices, add_over(): lax.all_to_all(x, axes, 0, 0, tiled=True, axis_index_groups=groups)  13 us
    all_to_all x1, starting transfers between devices, copy_over(): lax.all_to_all(spread, axes, 0, 0, tiled=True, axis_index_groups=groups)  11.8 us
    all_to_all x1, blocking collectives, per_device(): lax.all_to_all(local, 'z', 0, 0, tiled=True, axis_index_groups=quads)  11 us
    all_to_all x1, blocking collectives, per_device(): got = lax.all_to_all(packed, 'x', 0, 0, tiled=True)  10.5 us
    all_to_all x1, blocking collectives, copy_over(): lax.all_to_all(spread, axes, 0, 0, tiled=True, axis_index_groups=groups)  10.4 us
    ppermute x3, starting transfers between devices, per_device(): lax.ppermute(amp, 'x', [(i, (i + k) % nx) for i in range(nx)])  9.2 us
  transfers between devices with their start and end apart: 6, of which 3 were waited for; matrix products, arithmetic and copies ran while one was open for 0% of the time, Pallas kernels for 5%

profile of v1, /device:TPU:1, one launch (start us, length us, event | category | flops | bytes accessed | tf_op | source)
XLA Modules:
  0.0 100.0 jit_solution(17161877156539544777)
XLA Ops:
  0.6 0.0 copy-start.1
  0.6 1.8 %shard_map.86 = f32[544,128]{1,0:T(8,128)} custom-call(bf16[64,128]{1,0:T(8,128)(2,1)} %bitcast.18, s32[1,128]{1,0:T(1,128)} %bitcast.19, f32[1,128]{1,0:T(1,128)} %bitcast.20, bf16[128,128]{1,0:T(8,128)(2,1)} %refs_3_.1, s32[128,128]{1,0:T(8,128)} %refs_4_.1), custom_call_target="tpu_custom_call" | custom-call | tf_op jit(solution)/shard_map/pallas_call | solution.py:282
  2.5 10.5 %all_to_all.54 = f32[4,136,128]{2,1,0:T(8,128)S(1)} all-to-all(f32[4,136,128]{2,1,0:T(8,128)} %bitcast.17), channel_id=1, replica_groups=mesh['x'=4,'z'=16,'y'=4,'core'=2] {'x'}, dimensions={0} | all-to-all | bytes 557056 | tf_op jit(solution)/shard_map/all_to_all | solution.py:303
  13.0 0.6 shard_map.87
  13.6 11.0 %all_to_all.55 = f32[4,80,128]{2,1,0:T(8,128)S(1)} all-to-all(f32[4,80,128]{2,1,0:T(8,128)S(1)} %bitcast.13), channel_id=1, replica_groups={{0,8,16,24},{32,40,48,56},{64,72,80,88},{96,104,112,120},{1,9,17,25},{3..., dimensions={0} | all-to-all | bytes 327680 | tf_op jit(solution)/shard_map/all_to_all | solution.py:309
  24.6 0.7 shard_map.88
  25.3 10.4 %all-to-all-start.2 = ((f32[4,80,128]{2,1,0:T(8,128)}), f32[4,80,128]{2,1,0:T(8,128)S(1)}, u32[]{:S(2)}, u32[]{:S(2)}) async-start(f32[4,80,128]{2,1,0:T(8,128)} %bitcast.7), calls=%async_computation.2 | async-start | bytes 327680 | tf_op jit(solution)/shard_map/all_to_all | solution.py:249
  35.6 0.0 copy-done.1
  35.7 0.0 copy-start
  35.7 3.8 %shard_map.89 = (bf16[512,1280]{1,0:T(8,128)(2,1)S(1)}, f32[128,128]{1,0:T(8,128)S(1)}, f32[128,128]{1,0:T(8,128)S(1)}, f32[128,128]{1,0:T(8,128)S(1)}, f32[512,...) custom-call(f32[544,128]{1,0:T(8,128)S(1)} %bitcast.12, s32[1,512]{1,0:T(1,128)S(1)} %bitcast.16), custom_call_target="tpu_custom_call" | custom-call | flops 2147483648 | bytes 2097152 | tf_op jit(solution)/shard_map/pallas_call | solution.py:282
  39.4 6.7 %all-to-all-done.2 = f32[4,80,128]{2,1,0:T(8,128)S(1)} async-done(((f32[4,80,128]{2,1,0:T(8,128)}), f32[4,80,128]{2,1,0:T(8,128)S(1)}, u32[]{:S(2)}, u32[]{:S(2)}) %all-to-all-start.2) | async-done | bytes 163872 | tf_op jit(solution)/shard_map/all_to_all | solution.py:249
  46.2 10.4 %all_to_all.56 = f32[4,80,128]{2,1,0:T(8,128)S(1)} all-to-all(f32[4,80,128]{2,1,0:T(8,128)S(1)} %broadcast_in_dim.24), channel_id=1, replica_groups={{0,8,16,24},{32,40,48,56},{64,72,80,88},{96,104,112,120},{1,9,17,25},{3..., dimensions={0} | all-to-all | bytes 327680 | tf_op jit(solution)/shard_map/all_to_all | solution.py:257
  56.6 0.0 copy-done
  56.6 5.0 %shard_map.90 = (f32[320,128]{1,0:T(8,128)S(1)}, f32[512,128]{1,0:T(8,128)}) custom-call(f32[320,128]{1,0:T(8,128)S(1)} %bitcast.15, f32[20,64,64]{2,1,0:T(8,128)S(1)} %copy-done, bf16[512,1280]{1,0:T(8,128)(2,1)S(1)} %get-tuple-element.32.wide_ref, f32[128,128]{1,0:T(8,128)S(1)} %get-tuple-element.33.noise_ref, f32[128,128]{1,0:T(8,128)S(1)} %get-tuple-element.34.hi_ref, ...), custom_call_target="tpu_custom_call" | custom-call | flops 2147483648 | bytes 2097152 | tf_op jit(solution)/shard_map/pallas_call | solution.py:282
  61.6 5.1 %all-to-all-start.4 = ((f32[64,8,128]{2,1,0:T(8,128)}), f32[64,8,128]{2,1,0:T(8,128)S(1)}, u32[]{:S(2)}, u32[]{:S(2)}) async-start(f32[64,8,128]{2,1,0:T(8,128)} %bitcast.10), calls=%async_computation.4 | async-start | bytes 524288 | tf_op jit(solution)/shard_map/all_to_all | solution.py:249
  66.7 4.3 %collective-permute-start.2 = (f32[320,128]{1,0:T(8,128)S(1)}, f32[320,128]{1,0:T(8,128)S(1)}, u32[]{:S(2)}, u32[]{:S(2)}) collective-permute-start(f32[320,128]{1,0:T(8,128)S(1)} %get-tuple-element.38.refs_0_), channel_id=1, source_target_pairs={{0,384},{128,0},{256,128},{384,256},{1,385},{129,1},{257,129},{385... | collective-permute-start | bytes 491528 | tf_op jit(solution)/shard_map/ppermute | solution.py:339
  71.0 2.3 %collective-permute-start.1 = (f32[320,128]{1,0:T(8,128)S(1)}, f32[320,128]{1,0:T(8,128)S(1)}, u32[]{:S(2)}, u32[]{:S(2)}) collective-permute-start(f32[320,128]{1,0:T(8,128)S(1)} %get-tuple-element.38.refs_0_), channel_id=1, source_target_pairs={{0,256},{128,384},{256,0},{384,128},{1,257},{129,385},{257,1},{385... | collective-permute-start | bytes 491528 | tf_op jit(solution)/shard_map/ppermute | solution.py:339
  73.3 2.6 %collective-permute-start = (f32[320,128]{1,0:T(8,128)S(1)}, f32[320,128]{1,0:T(8,128)S(1)}, u32[]{:S(2)}, u32[]{:S(2)}) collective-permute-start(f32[320,128]{1,0:T(8,128)S(1)} %get-tuple-element.38.refs_0_), channel_id=1, source_target_pairs={{0,128},{128,256},{256,384},{384,0},{1,129},{129,257},{257,385},{3... | collective-permute-start | bytes 491528 | tf_op jit(solution)/shard_map/ppermute | solution.py:339
  75.9 6.3 %all-to-all-done.4 = f32[64,8,128]{2,1,0:T(8,128)S(1)} async-done(((f32[64,8,128]{2,1,0:T(8,128)}), f32[64,8,128]{2,1,0:T(8,128)S(1)}, u32[]{:S(2)}, u32[]{:S(2)}) %all-to-all-start.4) | async-done | bytes 262176 | tf_op jit(solution)/shard_map/all_to_all | solution.py:249
  82.2 0.1 reduce_sum.28
  82.2 0.0 collective-permute-done.2.refs_3_
  82.3 0.0 collective-permute-done.1.refs_2_
  82.3 0.0 collective-permute-done.refs_1_
  82.3 0.6 broadcast_in_dim.25
  82.9 11.8 %all-to-all-start.5 = ((f32[8,8,128]{2,1,0:T(8,128)}), f32[8,8,128]{2,1,0:T(8,128)S(1)}, u32[]{:S(2)}, u32[]{:S(2)}) async-start(f32[8,8,128]{2,1,0:T(8,128)} %broadcast_in_dim.25), calls=%async_computation.5 | async-start | bytes 65536 | tf_op jit(solution)/shard_map/all_to_all | solution.py:257
  94.7 1.6 %shard_map.91 = f32[1280,128]{1,0:T(8,128)} custom-call(f32[320,128]{1,0:T(8,128)S(1)} %get-tuple-element.38.refs_0_, f32[320,128]{1,0:T(8,128)S(1)} %collective-permute-done.refs_1_, f32[320,128]{1,0:T(8,128)S(1)} %collective-permute-done.1.refs_2_, f32[320,128]{1,0:T(8,128)S(1)} %collective-permute-done.2.refs_3_), custom_call_target="tpu_custom_call" | custom-call | tf_op jit(solution)/shard_map/pallas_call | solution.py:282
  96.3 3.1 %all-to-all-done.5 = f32[8,8,128]{2,1,0:T(8,128)S(1)} async-done(((f32[8,8,128]{2,1,0:T(8,128)}), f32[8,8,128]{2,1,0:T(8,128)S(1)}, u32[]{:S(2)}, u32[]{:S(2)}) %all-to-all-start.5) | async-done | bytes 32800 | tf_op jit(solution)/shard_map/all_to_all | solution.py:257
  99.4 0.6 reduce_sum.29
  (2 shorter events, 0.0 us)
Async XLA Ops:
  0.6 35.0 %copy-start.1 = (s32[512]{0:T(512)S(1)}, s32[512]{0:T(512)}, u32[]{:S(2)}) copy-start(s32[512]{0:T(512)} %param.13) | copy-start | bytes 6148
  25.3 20.9 %all-to-all-start.2 = ((f32[4,80,128]{2,1,0:T(8,128)}), f32[4,80,128]{2,1,0:T(8,128)S(1)}, u32[]{:S(2)}, u32[]{:S(2)}) async-start(f32[4,80,128]{2,1,0:T(8,128)} %bitcast.7), calls=%async_computation.2 | async-start | bytes 327680 | tf_op jit(solution)/shard_map/all_to_all | solution.py:249
  35.7 20.9 %copy-start = (f32[20,64,64]{2,1,0:T(8,128)S(1)}, f32[20,64,64]{2,1,0:T(8,128)}, u32[]{:S(2)}) copy-start(f32[20,64,64]{2,1,0:T(8,128)} %mix_ref.1) | copy-start | bytes 983044
  61.6 20.6 %all-to-all-start.4 = ((f32[64,8,128]{2,1,0:T(8,128)}), f32[64,8,128]{2,1,0:T(8,128)S(1)}, u32[]{:S(2)}, u32[]{:S(2)}) async-start(f32[64,8,128]{2,1,0:T(8,128)} %bitcast.10), calls=%async_computation.4 | async-start | bytes 524288 | tf_op jit(solution)/shard_map/all_to_all | solution.py:249
  66.7 15.6 %collective-permute-start.2 = (f32[320,128]{1,0:T(8,128)S(1)}, f32[320,128]{1,0:T(8,128)S(1)}, u32[]{:S(2)}, u32[]{:S(2)}) collective-permute-start(f32[320,128]{1,0:T(8,128)S(1)} %get-tuple-element.38.refs_0_), channel_id=1, source_target_pairs={{0,384},{128,0},{256,128},{384,256},{1,385},{129,1},{257,129},{385... | collective-permute-start | bytes 491528 | tf_op jit(solution)/shard_map/ppermute | solution.py:339
  71.0 11.2 %collective-permute-start.1 = (f32[320,128]{1,0:T(8,128)S(1)}, f32[320,128]{1,0:T(8,128)S(1)}, u32[]{:S(2)}, u32[]{:S(2)}) collective-permute-start(f32[320,128]{1,0:T(8,128)S(1)} %get-tuple-element.38.refs_0_), channel_id=1, source_target_pairs={{0,256},{128,384},{256,0},{384,128},{1,257},{129,385},{257,1},{385... | collective-permute-start | bytes 491528 | tf_op jit(solution)/shard_map/ppermute | solution.py:339
  73.3 9.0 %collective-permute-start = (f32[320,128]{1,0:T(8,128)S(1)}, f32[320,128]{1,0:T(8,128)S(1)}, u32[]{:S(2)}, u32[]{:S(2)}) collective-permute-start(f32[320,128]{1,0:T(8,128)S(1)} %get-tuple-element.38.refs_0_), channel_id=1, source_target_pairs={{0,128},{128,256},{256,384},{384,0},{1,129},{129,257},{257,385},{3... | collective-permute-start | bytes 491528 | tf_op jit(solution)/shard_map/ppermute | solution.py:339
  82.9 16.5 %all-to-all-start.5 = ((f32[8,8,128]{2,1,0:T(8,128)}), f32[8,8,128]{2,1,0:T(8,128)S(1)}, u32[]{:S(2)}, u32[]{:S(2)}) async-start(f32[8,8,128]{2,1,0:T(8,128)} %broadcast_in_dim.25), calls=%async_computation.5 | async-start | bytes 65536 | tf_op jit(solution)/shard_map/all_to_all | solution.py:257

commit v2 on v1

--- a/solution.py
+++ b/solution.py
@@ -120,7 +120,7 @@
         acc_ref[HALF:, :] += added[:, TILE_PIX:]
         return carry
 
-    lax.fori_loop(0, dets // GROUP, body, 0, unroll=4)
+    lax.fori_loop(0, dets // GROUP, body, 0, unroll=True)
 
 
 def sum_kernel(count, parts_ref, out_ref):
@@ -205,11 +205,12 @@
         p = jnp.concatenate(pieces, axis=0)
         mh, ml = split(mix_ref[b])
         ph, plow = split(p)
-        amp = p + jnp.dot(
-            jnp.concatenate([mh, ml, mh], axis=1),
-            jnp.concatenate([ph, ph, plow], axis=0),
+        mixed = jnp.dot(
+            jnp.concatenate([mh, ml], axis=0),
+            jnp.concatenate([ph, plow], axis=1),
             preferred_element_type=F32,
         )
+        amp = p + (mixed[:modes, :128] + (mixed[:modes, 128:] + mixed[modes:, :128]))
         rounded.append(amp.astype(BF16))
         packed = amp[:per, :]
         for j in range(1, nx):
@@ -323,7 +324,7 @@
     share, wide, noise, hi, lo, start, place = lax.optimization_barrier(
         (share, wide, noise, hi, lo, start, place)
     )
-    projected = copy_over(share, "z", quads)
+    projected = lax.all_gather(share, "z", axis=0, tiled=True, axis_index_groups=quads)
     amp, part = call(
         functools.partial(correct_kernel, nx, nl, bands),
         [(bands * modes // nx, 128), (tiles, TILE_PIX)],
@@ -338,9 +339,12 @@
     moved = [
         lax.ppermute(amp, "x", [(i, (i + k) % nx) for i in range(nx)]) for k in range(1, nx)
     ]
-    share = add_over(part, ("x", "z"))
-    share, *moved = lax.optimization_barrier((share, *moved))
-    sky_map = copy_over(share, ("y", "core")).reshape((nt,) + share.shape).sum(0)
+    swapped = lax.all_to_all(part, ("x", "z"), 0, 0, tiled=True)
+    swapped, *moved = lax.optimization_barrier((swapped, *moved))
+    (copies,) = call(
+        functools.partial(sum_kernel, nx * nz), [(nt * tiles // (nx * nz), TILE_PIX)], (swapped,)
+    )
+    sky_map = add_over(copies, ("y", "core"))
     (amplitudes,) = call(
         functools.partial(gather_kernel, nx, bands), [(bands * modes, times)], (amp, *moved)
     )

time: 101 us -> 105 us (1.040)
  blocking collectives: 31.8 us -> 34.2 us
  starting transfers between devices: 36.5 us -> 38.8 us
    all_gather x0 -> x1, blocking collectives: none -> 12.7 us  [per_device(): lax.all_gather(share, 'z', axis=0, tiled=True, axis_index_groups=quads)]
    all_to_all x1 -> x0, blocking collectives: 10.4 us -> none  [copy_over(): lax.all_to_all(spread, axes, 0, 0, tiled=True, axis_index_groups=groups)]
    all_to_all x2, starting transfers between devices: 15.5 us -> 23.8 us  [add_over(): lax.all_to_all(x, axes, 0, 0, tiled=True, axis_index_groups=groups)]
    all_to_all x1, starting transfers between devices: 11.8 us -> 5.8 us  [per_device(): swapped = lax.all_to_all(part, ('x', 'z'), 0, 0, tiled=True)]
    ppermute x3, waiting for transfers between devices: 0.01 us -> 5.36 us  [per_device(): lax.ppermute(amp, 'x', [(i, (i + k) % nx) for i in range(nx)])]
    all_to_all x2, waiting for transfers between devices: 13 us -> 10.7 us  [add_over(): lax.all_to_all(x, axes, 0, 0, tiled=True, axis_index_groups=groups)]
    all_to_all x1, waiting for transfers between devices: 3.13 us -> 0.91 us  [per_device(): swapped = lax.all_to_all(part, ('x', 'z'), 0, 0, tiled=True)]
    pallas_call x6 -> x7, Pallas kernels: 13.5 us -> 13.5 us  [call(): pl.pallas_call(kernel, out_shape=tuple((jax.ShapeDtypeStruct(s, t) for s,...]
  transfers between devices with their start and end apart: 6 -> 6, of which waited for: 3 -> 5; matrix products, arithmetic and copies ran while one was open for 0% -> 0% of each run, Pallas kernels for 5% -> 4%
where the time goes in v2:
time: 105 us
  starting transfers between devices  38.8 us (37%)
  blocking collectives  34.2 us (33%)
  waiting for transfers between devices  17 us (16%)
  Pallas kernels  13.5 us (13%)
    all_to_all x2, starting transfers between devices, add_over(): lax.all_to_all(x, axes, 0, 0, tiled=True, axis_index_groups=groups)  23.8 us
    pallas_call x7, Pallas kernels, call(): pl.pallas_call(kernel, out_shape=tuple((jax.ShapeDtypeStruct(s, t) for s,...  13.5 us
    all_gather x1, blocking collectives, per_device(): lax.all_gather(share, 'z', axis=0, tiled=True, axis_index_groups=quads)  12.7 us
    all_to_all x1, blocking collectives, per_device(): lax.all_to_all(local, 'z', 0, 0, tiled=True, axis_index_groups=quads)  11 us
    all_to_all x2, waiting for transfers between devices, add_over(): lax.all_to_all(x, axes, 0, 0, tiled=True, axis_index_groups=groups)  10.7 us
    all_to_all x1, blocking collectives, per_device(): got = lax.all_to_all(packed, 'x', 0, 0, tiled=True)  10.5 us
    ppermute x3, starting transfers between devices, per_device(): lax.ppermute(amp, 'x', [(i, (i + k) % nx) for i in range(nx)])  9.2 us
    all_to_all x1, starting transfers between devices, per_device(): swapped = lax.all_to_all(part, ('x', 'z'), 0, 0, tiled=True)  5.8 us
  transfers between devices with their start and end apart: 6, of which 5 were waited for; matrix products, arithmetic and copies ran while one was open for 0% of the time, Pallas kernels for 4%

profile of v2, /device:TPU:1, one launch (start us, length us, event | category | flops | bytes accessed | tf_op | source)
XLA Modules:
  0.0 104.8 jit_solution(11152183627184636233)
XLA Ops:
  0.6 0.0 copy-start.1
  0.6 1.8 %shard_map.86 = f32[544,128]{1,0:T(8,128)} custom-call(bf16[64,128]{1,0:T(8,128)(2,1)} %bitcast.19, s32[1,128]{1,0:T(1,128)} %bitcast.20, f32[1,128]{1,0:T(1,128)} %bitcast.21, bf16[128,128]{1,0:T(8,128)(2,1)} %refs_3_.1, s32[128,128]{1,0:T(8,128)} %refs_4_.1), custom_call_target="tpu_custom_call" | custom-call | tf_op jit(solution)/shard_map/pallas_call | solution.py:283
  2.5 10.5 %all_to_all.52 = f32[4,136,128]{2,1,0:T(8,128)S(1)} all-to-all(f32[4,136,128]{2,1,0:T(8,128)} %bitcast.18), channel_id=1, replica_groups=mesh['x'=4,'z'=16,'y'=4,'core'=2] {'x'}, dimensions={0} | all-to-all | bytes 557056 | tf_op jit(solution)/shard_map/all_to_all | solution.py:304
  13.0 0.6 shard_map.87
  13.6 11.0 %all_to_all.53 = f32[4,80,128]{2,1,0:T(8,128)S(1)} all-to-all(f32[4,80,128]{2,1,0:T(8,128)S(1)} %bitcast.15), channel_id=1, replica_groups={{0,8,16,24},{32,40,48,56},{64,72,80,88},{96,104,112,120},{1,9,17,25},{3..., dimensions={0} | all-to-all | bytes 327680 | tf_op jit(solution)/shard_map/all_to_all | solution.py:310
  24.6 0.7 shard_map.88
  25.3 10.4 %all-to-all-start.2 = ((f32[4,80,128]{2,1,0:T(8,128)}), f32[4,80,128]{2,1,0:T(8,128)S(1)}, u32[]{:S(2)}, u32[]{:S(2)}) async-start(f32[4,80,128]{2,1,0:T(8,128)} %bitcast.7), calls=%async_computation.2 | async-start | bytes 327680 | tf_op jit(solution)/shard_map/all_to_all | solution.py:250
  35.6 0.0 copy-done.1
  35.7 0.0 copy-start
  35.7 2.9 %shard_map.89 = (bf16[512,1280]{1,0:T(8,128)(2,1)S(1)}, f32[128,128]{1,0:T(8,128)S(1)}, f32[128,128]{1,0:T(8,128)S(1)}, f32[128,128]{1,0:T(8,128)S(1)}, f32[512,...) custom-call(f32[544,128]{1,0:T(8,128)S(1)} %bitcast.13, s32[1,512]{1,0:T(1,128)S(1)} %bitcast.17), custom_call_target="tpu_custom_call" | custom-call | flops 2147483648 | bytes 2097152 | tf_op jit(solution)/shard_map/pallas_call | solution.py:283
  38.6 7.6 %all-to-all-done.2 = f32[4,80,128]{2,1,0:T(8,128)S(1)} async-done(((f32[4,80,128]{2,1,0:T(8,128)}), f32[4,80,128]{2,1,0:T(8,128)S(1)}, u32[]{:S(2)}, u32[]{:S(2)}) %all-to-all-start.2) | async-done | bytes 163872 | tf_op jit(solution)/shard_map/all_to_all | solution.py:250
  46.2 12.7 %all_gather.3.proj_ref = f32[320,128]{1,0:T(8,128)S(1)} all-gather(f32[80,128]{1,0:T(8,128)S(1)} %reduce_sum.18), channel_id=1, replica_groups={{0,8,16,24},{32,40,48,56},{64,72,80,88},{96,104,112,120},{1,9,17,25},{3..., dimensions={0}, use_global_device_ids=true | all-gather | bytes 204800 | tf_op jit(solution)/shard_map/all_gather | solution.py:327
  58.9 0.0 copy-done
  58.9 5.2 %shard_map.90 = (f32[320,128]{1,0:T(8,128)S(1)}, f32[512,128]{1,0:T(8,128)}) custom-call(f32[320,128]{1,0:T(8,128)S(1)} %all_gather.3.proj_ref, f32[20,64,64]{2,1,0:T(8,128)S(1)} %copy-done, bf16[512,1280]{1,0:T(8,128)(2,1)S(1)} %get-tuple-element.32.wide_ref, f32[128,128]{1,0:T(8,128)S(1)} %get-tuple-element.33.noise_ref, ...), custom_call_target="tpu_custom_call" | custom-call | flops 2147483648 | bytes 2097152 | tf_op jit(solution)/shard_map/pallas_call | solution.py:283
  64.1 5.8 %all-to-all-start.3 = ((f32[64,8,128]{2,1,0:T(8,128)}), f32[64,8,128]{2,1,0:T(8,128)S(1)}, u32[]{:S(2)}, u32[]{:S(2)}) async-start(f32[64,8,128]{2,1,0:T(8,128)} %bitcast.9), calls=%async_computation.3 | async-start | bytes 524288 | tf_op jit(solution)/shard_map/all_to_all | solution.py:342
  69.9 4.3 %collective-permute-start.2 = (f32[320,128]{1,0:T(8,128)S(1)}, f32[320,128]{1,0:T(8,128)S(1)}, u32[]{:S(2)}, u32[]{:S(2)}) collective-permute-start(f32[320,128]{1,0:T(8,128)S(1)} %get-tuple-element.38.refs_0_), channel_id=1, source_target_pairs={{0,384},{128,0},{256,128},{384,256},{1,385},{129,1},{257,129},{385... | collective-permute-start | bytes 491528 | tf_op jit(solution)/shard_map/ppermute | solution.py:340
  74.3 2.3 %collective-permute-start.1 = (f32[320,128]{1,0:T(8,128)S(1)}, f32[320,128]{1,0:T(8,128)S(1)}, u32[]{:S(2)}, u32[]{:S(2)}) collective-permute-start(f32[320,128]{1,0:T(8,128)S(1)} %get-tuple-element.38.refs_0_), channel_id=1, source_target_pairs={{0,256},{128,384},{256,0},{384,128},{1,257},{129,385},{257,1},{385... | collective-permute-start | bytes 491528 | tf_op jit(solution)/shard_map/ppermute | solution.py:340
  76.6 2.6 %collective-permute-start = (f32[320,128]{1,0:T(8,128)S(1)}, f32[320,128]{1,0:T(8,128)S(1)}, u32[]{:S(2)}, u32[]{:S(2)}) collective-permute-start(f32[320,128]{1,0:T(8,128)S(1)} %get-tuple-element.38.refs_0_), channel_id=1, source_target_pairs={{0,128},{128,256},{256,384},{384,0},{1,129},{129,257},{257,385},{3... | collective-permute-start | bytes 491528 | tf_op jit(solution)/shard_map/ppermute | solution.py:340
  79.2 0.0 collective-permute-done.2.refs_3_
  79.2 3.1 %collective-permute-done.1.refs_2_ = f32[320,128]{1,0:T(8,128)S(1)} collective-permute-done((f32[320,128]{1,0:T(8,128)S(1)}, f32[320,128]{1,0:T(8,128)S(1)}, u32[]{:S(2)}, u32[]{:S(2)}) %collective-permute-start.1) | collective-permute-done | bytes 163872 | tf_op jit(solution)/shard_map/ppermute | solution.py:340
  82.3 2.2 %collective-permute-done.refs_1_ = f32[320,128]{1,0:T(8,128)S(1)} collective-permute-done((f32[320,128]{1,0:T(8,128)S(1)}, f32[320,128]{1,0:T(8,128)S(1)}, u32[]{:S(2)}, u32[]{:S(2)}) %collective-permute-start) | collective-permute-done | bytes 163872 | tf_op jit(solution)/shard_map/ppermute | solution.py:340
  84.5 0.9 all-to-all-done.3
  85.4 0.7 shard_map.92
  86.1 13.4 %all-to-all-start.4 = ((f32[8,8,128]{2,1,0:T(8,128)}), f32[8,8,128]{2,1,0:T(8,128)S(1)}, u32[]{:S(2)}, u32[]{:S(2)}) async-start(f32[8,8,128]{2,1,0:T(8,128)} %bitcast.11), calls=%async_computation.4 | async-start | bytes 65536 | tf_op jit(solution)/shard_map/all_to_all | solution.py:250
  99.5 1.6 %shard_map.91 = f32[1280,128]{1,0:T(8,128)} custom-call(f32[320,128]{1,0:T(8,128)S(1)} %get-tuple-element.38.refs_0_, f32[320,128]{1,0:T(8,128)S(1)} %collective-permute-done.refs_1_, f32[320,128]{1,0:T(8,128)S(1)} %collective-permute-done.1.refs_2_, f32[320,128]{1,0:T(8,128)S(1)} %collective-permute-done.2.refs_3_), custom_call_target="tpu_custom_call" | custom-call | tf_op jit(solution)/shard_map/pallas_call | solution.py:283
  101.1 3.1 %all-to-all-done.4 = f32[8,8,128]{2,1,0:T(8,128)S(1)} async-done(((f32[8,8,128]{2,1,0:T(8,128)}), f32[8,8,128]{2,1,0:T(8,128)S(1)}, u32[]{:S(2)}, u32[]{:S(2)}) %all-to-all-start.4) | async-done | bytes 32800 | tf_op jit(solution)/shard_map/all_to_all | solution.py:250
  104.2 0.6 reduce_sum.19
  (1 shorter events, 0.0 us)
Async XLA Ops:
  0.6 35.0 %copy-start.1 = (s32[512]{0:T(512)S(1)}, s32[512]{0:T(512)}, u32[]{:S(2)}) copy-start(s32[512]{0:T(512)} %param.13) | copy-start | bytes 6148
  25.3 20.9 %all-to-all-start.2 = ((f32[4,80,128]{2,1,0:T(8,128)}), f32[4,80,128]{2,1,0:T(8,128)S(1)}, u32[]{:S(2)}, u32[]{:S(2)}) async-start(f32[4,80,128]{2,1,0:T(8,128)} %bitcast.7), calls=%async_computation.2 | async-start | bytes 327680 | tf_op jit(solution)/shard_map/all_to_all | solution.py:250
  35.7 23.3 %copy-start = (f32[20,64,64]{2,1,0:T(8,128)S(1)}, f32[20,64,64]{2,1,0:T(8,128)}, u32[]{:S(2)}) copy-start(f32[20,64,64]{2,1,0:T(8,128)} %mix_ref.1) | copy-start | bytes 983044
  64.1 21.3 %all-to-all-start.3 = ((f32[64,8,128]{2,1,0:T(8,128)}), f32[64,8,128]{2,1,0:T(8,128)S(1)}, u32[]{:S(2)}, u32[]{:S(2)}) async-start(f32[64,8,128]{2,1,0:T(8,128)} %bitcast.9), calls=%async_computation.3 | async-start | bytes 524288 | tf_op jit(solution)/shard_map/all_to_all | solution.py:342
  69.9 9.2 %collective-permute-start.2 = (f32[320,128]{1,0:T(8,128)S(1)}, f32[320,128]{1,0:T(8,128)S(1)}, u32[]{:S(2)}, u32[]{:S(2)}) collective-permute-start(f32[320,128]{1,0:T(8,128)S(1)} %get-tuple-element.38.refs_0_), channel_id=1, source_target_pairs={{0,384},{128,0},{256,128},{384,256},{1,385},{129,1},{257,129},{385... | collective-permute-start | bytes 491528 | tf_op jit(solution)/shard_map/ppermute | solution.py:340
  74.3 8.0 %collective-permute-start.1 = (f32[320,128]{1,0:T(8,128)S(1)}, f32[320,128]{1,0:T(8,128)S(1)}, u32[]{:S(2)}, u32[]{:S(2)}) collective-permute-start(f32[320,128]{1,0:T(8,128)S(1)} %get-tuple-element.38.refs_0_), channel_id=1, source_target_pairs={{0,256},{128,384},{256,0},{384,128},{1,257},{129,385},{257,1},{385... | collective-permute-start | bytes 491528 | tf_op jit(solution)/shard_map/ppermute | solution.py:340
  76.6 8.0 %collective-permute-start = (f32[320,128]{1,0:T(8,128)S(1)}, f32[320,128]{1,0:T(8,128)S(1)}, u32[]{:S(2)}, u32[]{:S(2)}) collective-permute-start(f32[320,128]{1,0:T(8,128)S(1)} %get-tuple-element.38.refs_0_), channel_id=1, source_target_pairs={{0,128},{128,256},{256,384},{384,0},{1,129},{129,257},{257,385},{3... | collective-permute-start | bytes 491528 | tf_op jit(solution)/shard_map/ppermute | solution.py:340
  86.1 18.1 %all-to-all-start.4 = ((f32[8,8,128]{2,1,0:T(8,128)}), f32[8,8,128]{2,1,0:T(8,128)S(1)}, u32[]{:S(2)}, u32[]{:S(2)}) async-start(f32[8,8,128]{2,1,0:T(8,128)} %bitcast.11), calls=%async_computation.4 | async-start | bytes 65536 | tf_op jit(solution)/shard_map/all_to_all | solution.py:250

commit v3 on v1

--- a/solution.py
+++ b/solution.py
@@ -9,7 +9,7 @@
 
 TILE_PIX = 128
 HALF = 256
-GROUP = 8
+GROUP = 16
 EXTRA = 8
 F32 = jnp.float32
 BF16 = jnp.bfloat16
@@ -120,7 +120,7 @@
         acc_ref[HALF:, :] += added[:, TILE_PIX:]
         return carry
 
-    lax.fori_loop(0, dets // GROUP, body, 0, unroll=4)
+    lax.fori_loop(0, dets // GROUP, body, 0, unroll=True)
 
 
 def sum_kernel(count, parts_ref, out_ref):

time: 101 us -> 101 us (level)
  transfers between devices with their start and end apart: 6 -> 6, of which waited for: 3 -> 3; matrix products, arithmetic and copies ran while one was open for 0% -> 0% of each run, Pallas kernels for 5% -> 4%
where the time goes in v3:
time: 101 us; the launch traced here: 100 us
  starting transfers between devices  36.5 us (36%)
  blocking collectives  31.8 us (31%)
  waiting for transfers between devices  17 us (17%)
  Pallas kernels  12.8 us (13%)
    all_to_all x2, starting transfers between devices, add_over(): lax.all_to_all(x, axes, 0, 0, tiled=True, axis_index_groups=groups)  15.5 us
    all_to_all x2, waiting for transfers between devices, add_over(): lax.all_to_all(x, axes, 0, 0, tiled=True, axis_index_groups=groups)  13.9 us
    pallas_call x6, Pallas kernels, call(): pl.pallas_call(kernel, out_shape=tuple((jax.ShapeDtypeStruct(s, t) for s,...  12.8 us
    all_to_all x1, starting transfers between devices, copy_over(): lax.all_to_all(spread, axes, 0, 0, tiled=True, axis_index_groups=groups)  11.8 us
    all_to_all x1, blocking collectives, per_device(): lax.all_to_all(local, 'z', 0, 0, tiled=True, axis_index_groups=quads)  11 us
    all_to_all x1, blocking collectives, per_device(): got = lax.all_to_all(packed, 'x', 0, 0, tiled=True)  10.5 us
    all_to_all x1, blocking collectives, copy_over(): lax.all_to_all(spread, axes, 0, 0, tiled=True, axis_index_groups=groups)  10.4 us
    ppermute x3, starting transfers between devices, per_device(): lax.ppermute(amp, 'x', [(i, (i + k) % nx) for i in range(nx)])  9.2 us
  transfers between devices with their start and end apart: 6, of which 3 were waited for; matrix products, arithmetic and copies ran while one was open for 0% of the time, Pallas kernels for 4%

profile of v3, /device:TPU:1, one launch (start us, length us, event | category | flops | bytes accessed | tf_op | source)
XLA Modules:
  0.0 100.2 jit_solution(11999350133908014222)
XLA Ops:
  0.6 0.0 copy-start.1
  0.6 1.8 %shard_map.86 = f32[544,128]{1,0:T(8,128)} custom-call(bf16[64,128]{1,0:T(8,128)(2,1)} %bitcast.18, s32[1,128]{1,0:T(1,128)} %bitcast.19, f32[1,128]{1,0:T(1,128)} %bitcast.20, bf16[128,128]{1,0:T(8,128)(2,1)} %refs_3_.1, s32[128,128]{1,0:T(8,128)} %refs_4_.1), custom_call_target="tpu_custom_call" | custom-call | tf_op jit(solution)/shard_map/pallas_call | solution.py:282
  2.5 10.5 %all_to_all.54 = f32[4,136,128]{2,1,0:T(8,128)S(1)} all-to-all(f32[4,136,128]{2,1,0:T(8,128)} %bitcast.17), channel_id=1, replica_groups=mesh['x'=4,'z'=16,'y'=4,'core'=2] {'x'}, dimensions={0} | all-to-all | bytes 557056 | tf_op jit(solution)/shard_map/all_to_all | solution.py:303
  13.0 0.6 shard_map.87
  13.6 11.0 %all_to_all.55 = f32[4,80,128]{2,1,0:T(8,128)S(1)} all-to-all(f32[4,80,128]{2,1,0:T(8,128)S(1)} %bitcast.13), channel_id=1, replica_groups={{0,8,16,24},{32,40,48,56},{64,72,80,88},{96,104,112,120},{1,9,17,25},{3..., dimensions={0} | all-to-all | bytes 327680 | tf_op jit(solution)/shard_map/all_to_all | solution.py:309
  24.6 0.7 shard_map.88
  25.3 10.4 %all-to-all-start.2 = ((f32[4,80,128]{2,1,0:T(8,128)}), f32[4,80,128]{2,1,0:T(8,128)S(1)}, u32[]{:S(2)}, u32[]{:S(2)}) async-start(f32[4,80,128]{2,1,0:T(8,128)} %bitcast.7), calls=%async_computation.2 | async-start | bytes 327680 | tf_op jit(solution)/shard_map/all_to_all | solution.py:249
  35.6 0.0 copy-done.1
  35.7 0.0 copy-start
  35.7 2.9 %shard_map.89 = (bf16[512,1280]{1,0:T(8,128)(2,1)S(1)}, f32[128,128]{1,0:T(8,128)S(1)}, f32[128,128]{1,0:T(8,128)S(1)}, f32[128,128]{1,0:T(8,128)S(1)}, f32[512,...) custom-call(f32[544,128]{1,0:T(8,128)S(1)} %bitcast.12, s32[1,512]{1,0:T(1,128)S(1)} %bitcast.16), custom_call_target="tpu_custom_call" | custom-call | flops 2147483648 | bytes 2097152 | tf_op jit(solution)/shard_map/pallas_call | solution.py:282
  38.6 7.6 %all-to-all-done.2 = f32[4,80,128]{2,1,0:T(8,128)S(1)} async-done(((f32[4,80,128]{2,1,0:T(8,128)}), f32[4,80,128]{2,1,0:T(8,128)S(1)}, u32[]{:S(2)}, u32[]{:S(2)}) %all-to-all-start.2) | async-done | bytes 163872 | tf_op jit(solution)/shard_map/all_to_all | solution.py:249
  46.2 10.4 %all_to_all.56 = f32[4,80,128]{2,1,0:T(8,128)S(1)} all-to-all(f32[4,80,128]{2,1,0:T(8,128)S(1)} %broadcast_in_dim.24), channel_id=1, replica_groups={{0,8,16,24},{32,40,48,56},{64,72,80,88},{96,104,112,120},{1,9,17,25},{3..., dimensions={0} | all-to-all | bytes 327680 | tf_op jit(solution)/shard_map/all_to_all | solution.py:257
  56.6 0.0 copy-done
  56.6 5.2 %shard_map.90 = (f32[320,128]{1,0:T(8,128)S(1)}, f32[512,128]{1,0:T(8,128)}) custom-call(f32[320,128]{1,0:T(8,128)S(1)} %bitcast.15, f32[20,64,64]{2,1,0:T(8,128)S(1)} %copy-done, bf16[512,1280]{1,0:T(8,128)(2,1)S(1)} %get-tuple-element.32.wide_ref, f32[128,128]{1,0:T(8,128)S(1)} %get-tuple-element.33.noise_ref, f32[128,128]{1,0:T(8,128)S(1)} %get-tuple-element.34.hi_ref, ...), custom_call_target="tpu_custom_call" | custom-call | flops 2147483648 | bytes 2097152 | tf_op jit(solution)/shard_map/pallas_call | solution.py:282
  61.7 5.1 %all-to-all-start.4 = ((f32[64,8,128]{2,1,0:T(8,128)}), f32[64,8,128]{2,1,0:T(8,128)S(1)}, u32[]{:S(2)}, u32[]{:S(2)}) async-start(f32[64,8,128]{2,1,0:T(8,128)} %bitcast.10), calls=%async_computation.4 | async-start | bytes 524288 | tf_op jit(solution)/shard_map/all_to_all | solution.py:249
  66.9 4.3 %collective-permute-start.2 = (f32[320,128]{1,0:T(8,128)S(1)}, f32[320,128]{1,0:T(8,128)S(1)}, u32[]{:S(2)}, u32[]{:S(2)}) collective-permute-start(f32[320,128]{1,0:T(8,128)S(1)} %get-tuple-element.38.refs_0_), channel_id=1, source_target_pairs={{0,384},{128,0},{256,128},{384,256},{1,385},{129,1},{257,129},{385... | collective-permute-start | bytes 491528 | tf_op jit(solution)/shard_map/ppermute | solution.py:339
  71.2 2.3 %collective-permute-start.1 = (f32[320,128]{1,0:T(8,128)S(1)}, f32[320,128]{1,0:T(8,128)S(1)}, u32[]{:S(2)}, u32[]{:S(2)}) collective-permute-start(f32[320,128]{1,0:T(8,128)S(1)} %get-tuple-element.38.refs_0_), channel_id=1, source_target_pairs={{0,256},{128,384},{256,0},{384,128},{1,257},{129,385},{257,1},{385... | collective-permute-start | bytes 491528 | tf_op jit(solution)/shard_map/ppermute | solution.py:339
  73.5 2.6 %collective-permute-start = (f32[320,128]{1,0:T(8,128)S(1)}, f32[320,128]{1,0:T(8,128)S(1)}, u32[]{:S(2)}, u32[]{:S(2)}) collective-permute-start(f32[320,128]{1,0:T(8,128)S(1)} %get-tuple-element.38.refs_0_), channel_id=1, source_target_pairs={{0,128},{128,256},{256,384},{384,0},{1,129},{129,257},{257,385},{3... | collective-permute-start | bytes 491528 | tf_op jit(solution)/shard_map/ppermute | solution.py:339
  76.1 6.3 %all-to-all-done.4 = f32[64,8,128]{2,1,0:T(8,128)S(1)} async-done(((f32[64,8,128]{2,1,0:T(8,128)}), f32[64,8,128]{2,1,0:T(8,128)S(1)}, u32[]{:S(2)}, u32[]{:S(2)}) %all-to-all-start.4) | async-done | bytes 262176 | tf_op jit(solution)/shard_map/all_to_all | solution.py:249
  82.4 0.1 reduce_sum.28
  82.4 0.0 collective-permute-done.2.refs_3_
  82.4 0.0 collective-permute-done.1.refs_2_
  82.5 0.0 collective-permute-done.refs_1_
  82.5 0.6 broadcast_in_dim.25
  83.1 11.8 %all-to-all-start.5 = ((f32[8,8,128]{2,1,0:T(8,128)}), f32[8,8,128]{2,1,0:T(8,128)S(1)}, u32[]{:S(2)}, u32[]{:S(2)}) async-start(f32[8,8,128]{2,1,0:T(8,128)} %broadcast_in_dim.25), calls=%async_computation.5 | async-start | bytes 65536 | tf_op jit(solution)/shard_map/all_to_all | solution.py:257
  94.9 1.6 %shard_map.91 = f32[1280,128]{1,0:T(8,128)} custom-call(f32[320,128]{1,0:T(8,128)S(1)} %get-tuple-element.38.refs_0_, f32[320,128]{1,0:T(8,128)S(1)} %collective-permute-done.refs_1_, f32[320,128]{1,0:T(8,128)S(1)} %collective-permute-done.1.refs_2_, f32[320,128]{1,0:T(8,128)S(1)} %collective-permute-done.2.refs_3_), custom_call_target="tpu_custom_call" | custom-call | tf_op jit(solution)/shard_map/pallas_call | solution.py:282
  96.5 3.1 %all-to-all-done.5 = f32[8,8,128]{2,1,0:T(8,128)S(1)} async-done(((f32[8,8,128]{2,1,0:T(8,128)}), f32[8,8,128]{2,1,0:T(8,128)S(1)}, u32[]{:S(2)}, u32[]{:S(2)}) %all-to-all-start.5) | async-done | bytes 32800 | tf_op jit(solution)/shard_map/all_to_all | solution.py:257
  99.6 0.6 reduce_sum.29
  (2 shorter events, 0.0 us)
Async XLA Ops:
  0.6 35.0 %copy-start.1 = (s32[512]{0:T(512)S(1)}, s32[512]{0:T(512)}, u32[]{:S(2)}) copy-start(s32[512]{0:T(512)} %param.13) | copy-start | bytes 6148
  25.3 20.9 %all-to-all-start.2 = ((f32[4,80,128]{2,1,0:T(8,128)}), f32[4,80,128]{2,1,0:T(8,128)S(1)}, u32[]{:S(2)}, u32[]{:S(2)}) async-start(f32[4,80,128]{2,1,0:T(8,128)} %bitcast.7), calls=%async_computation.2 | async-start | bytes 327680 | tf_op jit(solution)/shard_map/all_to_all | solution.py:249
  35.7 20.9 %copy-start = (f32[20,64,64]{2,1,0:T(8,128)S(1)}, f32[20,64,64]{2,1,0:T(8,128)}, u32[]{:S(2)}) copy-start(f32[20,64,64]{2,1,0:T(8,128)} %mix_ref.1) | copy-start | bytes 983044
  61.7 20.6 %all-to-all-start.4 = ((f32[64,8,128]{2,1,0:T(8,128)}), f32[64,8,128]{2,1,0:T(8,128)S(1)}, u32[]{:S(2)}, u32[]{:S(2)}) async-start(f32[64,8,128]{2,1,0:T(8,128)} %bitcast.10), calls=%async_computation.4 | async-start | bytes 524288 | tf_op jit(solution)/shard_map/all_to_all | solution.py:249
  66.9 15.6 %collective-permute-start.2 = (f32[320,128]{1,0:T(8,128)S(1)}, f32[320,128]{1,0:T(8,128)S(1)}, u32[]{:S(2)}, u32[]{:S(2)}) collective-permute-start(f32[320,128]{1,0:T(8,128)S(1)} %get-tuple-element.38.refs_0_), channel_id=1, source_target_pairs={{0,384},{128,0},{256,128},{384,256},{1,385},{129,1},{257,129},{385... | collective-permute-start | bytes 491528 | tf_op jit(solution)/shard_map/ppermute | solution.py:339
  71.2 11.2 %collective-permute-start.1 = (f32[320,128]{1,0:T(8,128)S(1)}, f32[320,128]{1,0:T(8,128)S(1)}, u32[]{:S(2)}, u32[]{:S(2)}) collective-permute-start(f32[320,128]{1,0:T(8,128)S(1)} %get-tuple-element.38.refs_0_), channel_id=1, source_target_pairs={{0,256},{128,384},{256,0},{384,128},{1,257},{129,385},{257,1},{385... | collective-permute-start | bytes 491528 | tf_op jit(solution)/shard_map/ppermute | solution.py:339
  73.5 9.0 %collective-permute-start = (f32[320,128]{1,0:T(8,128)S(1)}, f32[320,128]{1,0:T(8,128)S(1)}, u32[]{:S(2)}, u32[]{:S(2)}) collective-permute-start(f32[320,128]{1,0:T(8,128)S(1)} %get-tuple-element.38.refs_0_), channel_id=1, source_target_pairs={{0,128},{128,256},{256,384},{384,0},{1,129},{129,257},{257,385},{3... | collective-permute-start | bytes 491528 | tf_op jit(solution)/shard_map/ppermute | solution.py:339
  83.1 16.5 %all-to-all-start.5 = ((f32[8,8,128]{2,1,0:T(8,128)}), f32[8,8,128]{2,1,0:T(8,128)S(1)}, u32[]{:S(2)}, u32[]{:S(2)}) async-start(f32[8,8,128]{2,1,0:T(8,128)} %broadcast_in_dim.25), calls=%async_computation.5 | async-start | bytes 65536 | tf_op jit(solution)/shard_map/all_to_all | solution.py:257

commit v4 on v3

--- a/solution.py
+++ b/solution.py
@@ -9,7 +9,6 @@
 
 TILE_PIX = 128
 HALF = 256
-GROUP = 16
 EXTRA = 8
 F32 = jnp.float32
 BF16 = jnp.bfloat16
@@ -95,7 +94,7 @@
     return jnp.broadcast_to(ref[pl.ds(i, 1), :], (16, times)).astype(BF16)[None]
 
 
-def add_bins(value_ref, hi_ref, lo_ref, acc_ref):
+def add_bins(value_ref, hi_ref, lo_ref, acc_ref, size, unroll):
     dets, times = value_ref.shape
     ids = lax.broadcasted_iota(jnp.int32, (HALF, times), 0).astype(F32).astype(BF16)
     ids = ids.reshape(HALF // 16, 16, times)
@@ -104,8 +103,8 @@
 
     def body(g, carry):
         left, right = [], []
-        for k in range(GROUP):
-            i = g * GROUP + k
+        for k in range(size):
+            i = g * size + k
             upper = row(hi_ref, i, times) == ids
             lower = row(lo_ref, i, times) == ids
             left.append(jnp.where(upper, one, zero).reshape(HALF, times))
@@ -120,16 +119,7 @@
         acc_ref[HALF:, :] += added[:, TILE_PIX:]
         return carry
 
-    lax.fori_loop(0, dets // GROUP, body, 0, unroll=True)
-
-
-def sum_kernel(count, parts_ref, out_ref):
-    rows = parts_ref.shape[0] // count
-    total = parts_ref[:rows, :]
-    for s in range(1, count):
-        total = total + parts_ref[s * rows:(s + 1) * rows, :]
-    for s in range(out_ref.shape[0] // rows):
-        out_ref[s * rows:(s + 1) * rows, :] = total
+    lax.fori_loop(0, dets // size, body, 0, unroll=unroll)
 
 
 def weighted_kernel(
@@ -175,7 +165,7 @@
     hi_ref[...] = (point >> 8).astype(F32)
     lo_ref[...] = (point & 255).astype(F32)
     acc_ref[...] = jnp.zeros_like(acc_ref)
-    add_bins(value_s, hi_ref, lo_ref, acc_ref)
+    add_bins(value_s, hi_ref, lo_ref, acc_ref, 16, True)
 
 
 def correct_kernel(
@@ -222,7 +212,7 @@
         fitted = jnp.where(group == s, fits[s * dets:(s + 1) * dets, :], fitted)
     value_s[...] = -(noise_ref[...] * fitted).astype(BF16).astype(F32)
     acc_s[...] = start_ref[...]
-    add_bins(value_s, hi_ref, lo_ref, acc_s)
+    add_bins(value_s, hi_ref, lo_ref, acc_s, 8, 4)
     high, low = split(acc_s[...])
     placed = jnp.dot(place_ref[...], jnp.concatenate([high, low], axis=1), preferred_element_type=F32)
     map_ref[...] = placed[:, :TILE_PIX] + placed[:, TILE_PIX:]
@@ -306,11 +296,8 @@
         [(bands * modes // nx, 128)],
         (got,),
     )
-    swapped = lax.all_to_all(local, "z", 0, 0, tiled=True, axis_index_groups=quads)
-    (copies,) = call(
-        functools.partial(sum_kernel, nl), [(nh * local.shape[0] // nl, 128)], (swapped,)
-    )
-    copies, got = lax.optimization_barrier((copies, got))
+    local, got = lax.optimization_barrier((local, got))
+    share = add_over(local, "z", quads)
     wide, noise, hi, lo, start, place = call(
         functools.partial(weighted_kernel, nx, bands, modes),
         [(nx * dets, bands * modes)] + [(dets, times)] * 3 + [(2 * HALF, TILE_PIX), (tiles, 2 * HALF)],
@@ -319,10 +306,10 @@
         cost=bin_cost,
         types=[BF16] + [F32] * 4 + [BF16],
     )
-    share = add_over(copies, "z", rings)
     share, wide, noise, hi, lo, start, place = lax.optimization_barrier(
         (share, wide, noise, hi, lo, start, place)
     )
+    share = copy_over(share, "z", rings).reshape((nh,) + share.shape).sum(0)
     projected = copy_over(share, "z", quads)
     amp, part = call(
         functools.partial(correct_kernel, nx, nl, bands),

time: 101 us -> 101 us (level)
  blocking collectives: 31.8 us -> 42.2 us
  waiting for transfers between devices: 17 us -> 11.4 us
  starting transfers between devices: 36.5 us -> 32.4 us
    all_to_all x1 -> x2, blocking collectives: 10.4 us -> 31.7 us  [copy_over(): lax.all_to_all(spread, axes, 0, 0, tiled=True, axis_index_groups=groups)]
    all_to_all x1 -> x0, blocking collectives: 11 us -> none  [per_device(): lax.all_to_all(local, 'z', 0, 0, tiled=True, axis_index_groups=quads)]
    all_to_all x2, waiting for transfers between devices: 13.9 us -> 8.22 us  [add_over(): lax.all_to_all(x, axes, 0, 0, tiled=True, axis_index_groups=groups)]
    all_to_all x2, starting transfers between devices: 15.5 us -> 12.1 us  [add_over(): lax.all_to_all(x, axes, 0, 0, tiled=True, axis_index_groups=groups)]
    pallas_call x6 -> x5, Pallas kernels: 12.8 us -> 12.5 us  [call(): pl.pallas_call(kernel, out_shape=tuple((jax.ShapeDtypeStruct(s, t) for s,...]
where the time goes in v4:
time: 101 us
  blocking collectives  42.2 us (42%)
  starting transfers between devices  32.4 us (32%)
  Pallas kernels  12.5 us (12%)
  waiting for transfers between devices  11.4 us (11%)
    all_to_all x2, blocking collectives, copy_over(): lax.all_to_all(spread, axes, 0, 0, tiled=True, axis_index_groups=groups)  31.7 us
    pallas_call x5, Pallas kernels, call(): pl.pallas_call(kernel, out_shape=tuple((jax.ShapeDtypeStruct(s, t) for s,...  12.5 us
    all_to_all x2, starting transfers between devices, add_over(): lax.all_to_all(x, axes, 0, 0, tiled=True, axis_index_groups=groups)  12.1 us
    all_to_all x1, starting transfers between devices, copy_over(): lax.all_to_all(spread, axes, 0, 0, tiled=True, axis_index_groups=groups)  11.2 us
    all_to_all x1, blocking collectives, per_device(): got = lax.all_to_all(packed, 'x', 0, 0, tiled=True)  10.5 us
    ppermute x3, starting transfers between devices, per_device(): lax.ppermute(amp, 'x', [(i, (i + k) % nx) for i in range(nx)])  9.2 us
    all_to_all x2, waiting for transfers between devices, add_over(): lax.all_to_all(x, axes, 0, 0, tiled=True, axis_index_groups=groups)  8.22 us
    all_to_all x1, waiting for transfers between devices, copy_over(): lax.all_to_all(spread, axes, 0, 0, tiled=True, axis_index_groups=groups)  3.13 us
  transfers between devices with their start and end apart: 6, of which 3 were waited for; matrix products, arithmetic and copies ran while one was open for 0% of the time, Pallas kernels for 4%

profile of v4, /device:TPU:1, one launch (start us, length us, event | category | flops | bytes accessed | tf_op | source)
XLA Modules:
  0.0 100.6 jit_solution(9511807954292269585)
XLA Ops:
  0.6 0.0 copy-start.1
  0.6 1.8 %shard_map.86 = f32[544,128]{1,0:T(8,128)} custom-call(bf16[64,128]{1,0:T(8,128)(2,1)} %bitcast.14, s32[1,128]{1,0:T(1,128)} %bitcast.15, f32[1,128]{1,0:T(1,128)} %bitcast.16, bf16[128,128]{1,0:T(8,128)(2,1)} %refs_3_.1, s32[128,128]{1,0:T(8,128)} %refs_4_.1), custom_call_target="tpu_custom_call" | custom-call | tf_op jit(solution)/shard_map/pallas_call | solution.py:272
  2.5 10.5 %all_to_all.49 = f32[4,136,128]{2,1,0:T(8,128)S(1)} all-to-all(f32[4,136,128]{2,1,0:T(8,128)} %bitcast.13), channel_id=1, replica_groups=mesh['x'=4,'z'=16,'y'=4,'core'=2] {'x'}, dimensions={0} | all-to-all | bytes 557056 | tf_op jit(solution)/shard_map/all_to_all | solution.py:293
  13.0 1.3 %shard_map.87 = f32[320,128]{1,0:T(8,128)} custom-call(f32[544,128]{1,0:T(8,128)S(1)} %bitcast.9), custom_call_target="tpu_custom_call" | custom-call | tf_op jit(solution)/shard_map/pallas_call | solution.py:272
  14.2 5.6 %all-to-all-start.1 = ((f32[4,80,128]{2,1,0:T(8,128)}), f32[4,80,128]{2,1,0:T(8,128)S(1)}, u32[]{:S(2)}, u32[]{:S(2)}) async-start(f32[4,80,128]{2,1,0:T(8,128)} %bitcast.5), calls=%async_computation.1 | async-start | bytes 327680 | tf_op jit(solution)/shard_map/all_to_all | solution.py:239
  19.9 0.0 copy-done.1
  19.9 2.9 %shard_map.88 = (bf16[512,1280]{1,0:T(8,128)(2,1)S(1)}, f32[128,128]{1,0:T(8,128)S(1)}, f32[128,128]{1,0:T(8,128)S(1)}, f32[128,128]{1,0:T(8,128)S(1)}, f32[512,...) custom-call(f32[544,128]{1,0:T(8,128)S(1)} %bitcast.10, s32[1,512]{1,0:T(1,128)S(1)} %bitcast.12), custom_call_target="tpu_custom_call" | custom-call | flops 2147483648 | bytes 2097152 | tf_op jit(solution)/shard_map/pallas_call | solution.py:272
  22.8 0.0 copy-start
  22.8 1.9 %all-to-all-done.1 = f32[4,80,128]{2,1,0:T(8,128)S(1)} async-done(((f32[4,80,128]{2,1,0:T(8,128)}), f32[4,80,128]{2,1,0:T(8,128)S(1)}, u32[]{:S(2)}, u32[]{:S(2)}) %all-to-all-start.1) | async-done | bytes 163872 | tf_op jit(solution)/shard_map/all_to_all | solution.py:239
  24.8 21.5 %all_to_all.50 = f32[4,80,128]{2,1,0:T(8,128)S(1)} all-to-all(f32[4,80,128]{2,1,0:T(8,128)S(1)} %broadcast_in_dim.30), channel_id=1, replica_groups={{0,32,80,112},{8,40,88,120},{16,48,64,96},{24,56,72,104},{1,33,81,113},..., dimensions={0} | all-to-all | bytes 327680 | tf_op jit(solution)/shard_map/all_to_all | solution.py:247
  46.3 10.2 %all_to_all.51 = f32[4,80,128]{2,1,0:T(8,128)S(1)} all-to-all(f32[4,80,128]{2,1,0:T(8,128)S(1)} %broadcast_in_dim.31), channel_id=1, replica_groups={{0,8,16,24},{32,40,48,56},{64,72,80,88},{96,104,112,120},{1,9,17,25},{3..., dimensions={0} | all-to-all | bytes 327680 | tf_op jit(solution)/shard_map/all_to_all | solution.py:247
  56.5 0.0 copy-done
  56.5 4.9 %shard_map.89 = (f32[320,128]{1,0:T(8,128)S(1)}, f32[512,128]{1,0:T(8,128)}) custom-call(f32[320,128]{1,0:T(8,128)S(1)} %bitcast.11, f32[20,64,64]{2,1,0:T(8,128)S(1)} %copy-done, bf16[512,1280]{1,0:T(8,128)(2,1)S(1)} %get-tuple-element.32.wide_ref, f32[128,128]{1,0:T(8,128)S(1)} %get-tuple-element.33.noise_ref, f32[128,128]{1,0:T(8,128)S(1)} %get-tuple-element.34.hi_ref, ...), custom_call_target="tpu_custom_call" | custom-call | flops 2147483648 | bytes 2097152 | tf_op jit(solution)/shard_map/pallas_call | solution.py:272
  61.5 6.4 %all-to-all-start.4 = ((f32[64,8,128]{2,1,0:T(8,128)}), f32[64,8,128]{2,1,0:T(8,128)S(1)}, u32[]{:S(2)}, u32[]{:S(2)}) async-start(f32[64,8,128]{2,1,0:T(8,128)} %bitcast.8), calls=%async_computation.4 | async-start | bytes 524288 | tf_op jit(solution)/shard_map/all_to_all | solution.py:239
  67.9 4.3 %collective-permute-start.2 = (f32[320,128]{1,0:T(8,128)S(1)}, f32[320,128]{1,0:T(8,128)S(1)}, u32[]{:S(2)}, u32[]{:S(2)}) collective-permute-start(f32[320,128]{1,0:T(8,128)S(1)} %get-tuple-element.38.refs_0_), channel_id=1, source_target_pairs={{0,384},{128,0},{256,128},{384,256},{1,385},{129,1},{257,129},{385... | collective-permute-start | bytes 491528 | tf_op jit(solution)/shard_map/ppermute | solution.py:326
  72.2 2.3 %collective-permute-start.1 = (f32[320,128]{1,0:T(8,128)S(1)}, f32[320,128]{1,0:T(8,128)S(1)}, u32[]{:S(2)}, u32[]{:S(2)}) collective-permute-start(f32[320,128]{1,0:T(8,128)S(1)} %get-tuple-element.38.refs_0_), channel_id=1, source_target_pairs={{0,256},{128,384},{256,0},{384,128},{1,257},{129,385},{257,1},{385... | collective-permute-start | bytes 491528 | tf_op jit(solution)/shard_map/ppermute | solution.py:326
  74.5 2.6 %collective-permute-start = (f32[320,128]{1,0:T(8,128)S(1)}, f32[320,128]{1,0:T(8,128)S(1)}, u32[]{:S(2)}, u32[]{:S(2)}) collective-permute-start(f32[320,128]{1,0:T(8,128)S(1)} %get-tuple-element.38.refs_0_), channel_id=1, source_target_pairs={{0,128},{128,256},{256,384},{384,0},{1,129},{129,257},{257,385},{3... | collective-permute-start | bytes 491528 | tf_op jit(solution)/shard_map/ppermute | solution.py:326
  77.1 6.3 %all-to-all-done.4 = f32[64,8,128]{2,1,0:T(8,128)S(1)} async-done(((f32[64,8,128]{2,1,0:T(8,128)}), f32[64,8,128]{2,1,0:T(8,128)S(1)}, u32[]{:S(2)}, u32[]{:S(2)}) %all-to-all-start.4) | async-done | bytes 262176 | tf_op jit(solution)/shard_map/all_to_all | solution.py:239
  83.4 0.1 reduce_sum.38
  83.5 0.0 collective-permute-done.2.refs_3_
  83.5 0.0 collective-permute-done.1.refs_2_
  83.5 0.0 collective-permute-done.refs_1_
  83.5 0.6 broadcast_in_dim.32
  84.1 11.2 %all-to-all-start.5 = ((f32[8,8,128]{2,1,0:T(8,128)}), f32[8,8,128]{2,1,0:T(8,128)S(1)}, u32[]{:S(2)}, u32[]{:S(2)}) async-start(f32[8,8,128]{2,1,0:T(8,128)} %broadcast_in_dim.32), calls=%async_computation.5 | async-start | bytes 65536 | tf_op jit(solution)/shard_map/all_to_all | solution.py:247
  95.3 1.6 %shard_map.90 = f32[1280,128]{1,0:T(8,128)} custom-call(f32[320,128]{1,0:T(8,128)S(1)} %get-tuple-element.38.refs_0_, f32[320,128]{1,0:T(8,128)S(1)} %collective-permute-done.refs_1_, f32[320,128]{1,0:T(8,128)S(1)} %collective-permute-done.1.refs_2_, f32[320,128]{1,0:T(8,128)S(1)} %collective-permute-done.2.refs_3_), custom_call_target="tpu_custom_call" | custom-call | tf_op jit(solution)/shard_map/pallas_call | solution.py:272
  96.9 3.1 %all-to-all-done.5 = f32[8,8,128]{2,1,0:T(8,128)S(1)} async-done(((f32[8,8,128]{2,1,0:T(8,128)}), f32[8,8,128]{2,1,0:T(8,128)S(1)}, u32[]{:S(2)}, u32[]{:S(2)}) %all-to-all-start.5) | async-done | bytes 32800 | tf_op jit(solution)/shard_map/all_to_all | solution.py:247
  100.0 0.6 reduce_sum.39
  (4 shorter events, 0.0 us)
Async XLA Ops:
  0.6 19.2 %copy-start.1 = (s32[512]{0:T(512)S(1)}, s32[512]{0:T(512)}, u32[]{:S(2)}) copy-start(s32[512]{0:T(512)} %param.13) | copy-start | bytes 6148
  14.2 10.5 %all-to-all-start.1 = ((f32[4,80,128]{2,1,0:T(8,128)}), f32[4,80,128]{2,1,0:T(8,128)S(1)}, u32[]{:S(2)}, u32[]{:S(2)}) async-start(f32[4,80,128]{2,1,0:T(8,128)} %bitcast.5), calls=%async_computation.1 | async-start | bytes 327680 | tf_op jit(solution)/shard_map/all_to_all | solution.py:239
  22.8 33.7 %copy-start = (f32[20,64,64]{2,1,0:T(8,128)S(1)}, f32[20,64,64]{2,1,0:T(8,128)}, u32[]{:S(2)}) copy-start(f32[20,64,64]{2,1,0:T(8,128)} %mix_ref.1) | copy-start | bytes 983044
  61.5 21.9 %all-to-all-start.4 = ((f32[64,8,128]{2,1,0:T(8,128)}), f32[64,8,128]{2,1,0:T(8,128)S(1)}, u32[]{:S(2)}, u32[]{:S(2)}) async-start(f32[64,8,128]{2,1,0:T(8,128)} %bitcast.8), calls=%async_computation.4 | async-start | bytes 524288 | tf_op jit(solution)/shard_map/all_to_all | solution.py:239
  67.9 15.6 %collective-permute-start.2 = (f32[320,128]{1,0:T(8,128)S(1)}, f32[320,128]{1,0:T(8,128)S(1)}, u32[]{:S(2)}, u32[]{:S(2)}) collective-permute-start(f32[320,128]{1,0:T(8,128)S(1)} %get-tuple-element.38.refs_0_), channel_id=1, source_target_pairs={{0,384},{128,0},{256,128},{384,256},{1,385},{129,1},{257,129},{385... | collective-permute-start | bytes 491528 | tf_op jit(solution)/shard_map/ppermute | solution.py:326
  72.2 11.2 %collective-permute-start.1 = (f32[320,128]{1,0:T(8,128)S(1)}, f32[320,128]{1,0:T(8,128)S(1)}, u32[]{:S(2)}, u32[]{:S(2)}) collective-permute-start(f32[320,128]{1,0:T(8,128)S(1)} %get-tuple-element.38.refs_0_), channel_id=1, source_target_pairs={{0,256},{128,384},{256,0},{384,128},{1,257},{129,385},{257,1},{385... | collective-permute-start | bytes 491528 | tf_op jit(solution)/shard_map/ppermute | solution.py:326
  74.5 9.0 %collective-permute-start = (f32[320,128]{1,0:T(8,128)S(1)}, f32[320,128]{1,0:T(8,128)S(1)}, u32[]{:S(2)}, u32[]{:S(2)}) collective-permute-start(f32[320,128]{1,0:T(8,128)S(1)} %get-tuple-element.38.refs_0_), channel_id=1, source_target_pairs={{0,128},{128,256},{256,384},{384,0},{1,129},{129,257},{257,385},{3... | collective-permute-start | bytes 491528 | tf_op jit(solution)/shard_map/ppermute | solution.py:326
  84.1 15.9 %all-to-all-start.5 = ((f32[8,8,128]{2,1,0:T(8,128)}), f32[8,8,128]{2,1,0:T(8,128)S(1)}, u32[]{:S(2)}, u32[]{:S(2)}) async-start(f32[8,8,128]{2,1,0:T(8,128)} %broadcast_in_dim.32), calls=%async_computation.5 | async-start | bytes 65536 | tf_op jit(solution)/shard_map/all_to_all | solution.py:247

commit v5 on v1

--- a/solution.py
+++ b/solution.py
@@ -133,8 +133,11 @@
 
 
 def weighted_kernel(
-    nx, bands, modes, got_ref, own_ref, wide_ref, noise_ref, hi_ref, lo_ref, acc_ref, place_ref, value_s
+    nx, bands, modes, got_ref, own_ref, mix_ref, parts_ref, wide_ref, noise_ref, hi_ref, lo_ref, acc_ref, place_ref, value_s
 ):
+    for b in range(bands):
+        mh, ml = split(mix_ref[b])
+        parts_ref[b * modes:(b + 1) * modes, :] = jnp.concatenate([mh, ml, mh], axis=1)
     tiles = place_ref.shape[0]
     own = own_ref[...]
     own = jnp.broadcast_to(((own & 1) * HALF + (own >> 1)).astype(F32), (128, tiles))
@@ -179,10 +182,10 @@
 
 
 def correct_kernel(
-    nx, owners, bands, proj_ref, mix_ref, wide_ref, noise_ref, hi_ref, lo_ref, start_ref, place_ref,
+    nx, owners, bands, proj_ref, parts_ref, wide_ref, noise_ref, hi_ref, lo_ref, start_ref, place_ref,
     amp_ref, map_ref, value_s, acc_s, shares_s
 ):
-    modes = mix_ref.shape[1]
+    modes = parts_ref.shape[0] // bands
     dets = noise_ref.shape[0]
     width = 128 // nx
     per = modes // nx
@@ -203,10 +206,9 @@
                 piece = jnp.where(group == g, turned[(g - j) % nx], piece)
             pieces.append(piece)
         p = jnp.concatenate(pieces, axis=0)
-        mh, ml = split(mix_ref[b])
         ph, plow = split(p)
         amp = p + jnp.dot(
-            jnp.concatenate([mh, ml, mh], axis=1),
+            parts_ref[b * modes:(b + 1) * modes, :],
             jnp.concatenate([ph, ph, plow], axis=0),
             preferred_element_type=F32,
         )
@@ -311,23 +313,23 @@
         functools.partial(sum_kernel, nl), [(nh * local.shape[0] // nl, 128)], (swapped,)
     )
     copies, got = lax.optimization_barrier((copies, got))
-    wide, noise, hi, lo, start, place = call(
+    parts, wide, noise, hi, lo, start, place = call(
         functools.partial(weighted_kernel, nx, bands, modes),
-        [(nx * dets, bands * modes)] + [(dets, times)] * 3 + [(2 * HALF, TILE_PIX), (tiles, 2 * HALF)],
-        (got, ownership[None, :]),
+        [(bands * modes, 3 * modes), (nx * dets, bands * modes)] + [(dets, times)] * 3 + [(2 * HALF, TILE_PIX), (tiles, 2 * HALF)],
+        (got, ownership[None, :], mode_mix),
         scratch=[pltpu.VMEM((dets, times), F32)],
         cost=bin_cost,
-        types=[BF16] + [F32] * 4 + [BF16],
+        types=[BF16] * 2 + [F32] * 4 + [BF16],
     )
     share = add_over(copies, "z", rings)
-    share, wide, noise, hi, lo, start, place = lax.optimization_barrier(
-        (share, wide, noise, hi, lo, start, place)
+    share, parts, wide, noise, hi, lo, start, place = lax.optimization_barrier(
+        (share, parts, wide, noise, hi, lo, start, place)
     )
     projected = copy_over(share, "z", quads)
     amp, part = call(
         functools.partial(correct_kernel, nx, nl, bands),
         [(bands * modes // nx, 128), (tiles, TILE_PIX)],
-        (projected, mode_mix, wide, noise, hi, lo, start, place),
+        (projected, parts, wide, noise, hi, lo, start, place),
         scratch=[
             pltpu.VMEM((dets, times), F32),
             pltpu.VMEM((2 * HALF, TILE_PIX), F32),

time: 101 us -> 105 us (1.040)
  local copies, waits for them, and re-layouts: 0.63 us -> 5.21 us
  waiting for transfers between devices: 16.1 us -> 14.3 us
    unnamed x4 -> x16, local copies, waits for them, and re-layouts: 0.01 us -> 4.58 us
    all_to_all x2, waiting for transfers between devices: 13 us -> 11.2 us  [add_over(): lax.all_to_all(x, axes, 0, 0, tiled=True, axis_index_groups=groups)]
where the time goes in v5:
time: 105 us; the launch traced here: 104 us
  starting transfers between devices  37 us (35%)
  blocking collectives  31.8 us (30%)
  waiting for transfers between devices  14.3 us (14%)
  Pallas kernels  13.5 us (13%)
  local copies, waits for them, and re-layouts  5.21 us (5%)
  other arithmetic  1.6 us (2%)
    all_to_all x2, starting transfers between devices, add_over(): lax.all_to_all(x, axes, 0, 0, tiled=True, axis_index_groups=groups)  16.4 us
    pallas_call x6, Pallas kernels, call(): pl.pallas_call(kernel, out_shape=tuple((jax.ShapeDtypeStruct(s, t) for s,...  13.5 us
    all_to_all x1, starting transfers between devices, copy_over(): lax.all_to_all(spread, axes, 0, 0, tiled=True, axis_index_groups=groups)  11.5 us
    all_to_all x2, waiting for transfers between devices, add_over(): lax.all_to_all(x, axes, 0, 0, tiled=True, axis_index_groups=groups)  11.2 us
    all_to_all x1, blocking collectives, per_device(): lax.all_to_all(local, 'z', 0, 0, tiled=True, axis_index_groups=quads)  11 us
    all_to_all x1, blocking collectives, per_device(): got = lax.all_to_all(packed, 'x', 0, 0, tiled=True)  10.5 us
    all_to_all x1, blocking collectives, copy_over(): lax.all_to_all(spread, axes, 0, 0, tiled=True, axis_index_groups=groups)  10.4 us
    ppermute x3, starting transfers between devices, per_device(): lax.ppermute(amp, 'x', [(i, (i + k) % nx) for i in range(nx)])  9.2 us
  transfers between devices with their start and end apart: 6, of which 3 were waited for; matrix products, arithmetic and copies ran while one was open for 0% of the time, Pallas kernels for 5%

profile of v5, /device:TPU:1, one launch (start us, length us, event | category | flops | bytes accessed | tf_op | source)
XLA Modules:
  0.0 104.2 jit_solution(10749570438766809129)
XLA Ops:
  0.7 1.9 %shard_map.86 = f32[544,128]{1,0:T(8,128)} custom-call(bf16[64,128]{1,0:T(8,128)(2,1)} %bitcast.18, s32[1,128]{1,0:T(1,128)} %bitcast.19, f32[1,128]{1,0:T(1,128)} %bitcast.20, bf16[128,128]{1,0:T(8,128)(2,1)} %refs_3_.1, s32[128,128]{1,0:T(8,128)} %refs_4_.1), custom_call_target="tpu_custom_call" | custom-call | tf_op jit(solution)/shard_map/pallas_call | solution.py:284
  2.6 10.5 %all_to_all.54 = f32[4,136,128]{2,1,0:T(8,128)S(1)} all-to-all(f32[4,136,128]{2,1,0:T(8,128)} %bitcast.17), channel_id=1, replica_groups=mesh['x'=4,'z'=16,'y'=4,'core'=2] {'x'}, dimensions={0} | all-to-all | bytes 557056 | tf_op jit(solution)/shard_map/all_to_all | solution.py:305
  13.0 0.6 shard_map.87
  13.6 11.0 %all_to_all.55 = f32[4,80,128]{2,1,0:T(8,128)S(1)} all-to-all(f32[4,80,128]{2,1,0:T(8,128)S(1)} %bitcast.13), channel_id=1, replica_groups={{0,8,16,24},{32,40,48,56},{64,72,80,88},{96,104,112,120},{1,9,17,25},{3..., dimensions={0} | all-to-all | bytes 327680 | tf_op jit(solution)/shard_map/all_to_all | solution.py:311
  24.6 0.7 shard_map.88
  25.3 10.4 %all-to-all-start.2 = ((f32[4,80,128]{2,1,0:T(8,128)}), f32[4,80,128]{2,1,0:T(8,128)}, u32[]{:S(2)}, u32[]{:S(2)}) async-start(f32[4,80,128]{2,1,0:T(8,128)} %bitcast.7), calls=%async_computation.2 | async-start | bytes 327680 | tf_op jit(solution)/shard_map/all_to_all | solution.py:251
  35.7 3.8 %shard_map.89 = (bf16[1280,192]{1,0:T(8,128)(2,1)S(1)}, bf16[512,1280]{1,0:T(8,128)(2,1)S(1)}, f32[128,128]{1,0:T(8,128)S(1)}, f32[128,128]{1,0:T(8,128)S(1)}, f...) custom-call(f32[544,128]{1,0:T(8,128)S(1)} %bitcast.12, s32[1,512]{1,0:T(1,128)S(1)} %bitcast.16, ...), custom_call_target="tpu_custom_call" | custom-call | flops 2147483648 | bytes 2097152 | tf_op jit(solution)/shard_map/pallas_call | solution.py:284
  39.5 0.0 copy-start.2
  39.5 0.7 copy-done.2
  40.2 0.6 copy-done.4
  40.8 0.6 copy-done.6
  41.5 4.9 %all-to-all-done.2 = f32[4,80,128]{2,1,0:T(8,128)} async-done(((f32[4,80,128]{2,1,0:T(8,128)}), f32[4,80,128]{2,1,0:T(8,128)}, u32[]{:S(2)}, u32[]{:S(2)}) %all-to-all-start.2) | async-done | bytes 163872 | tf_op jit(solution)/shard_map/all_to_all | solution.py:251
  46.3 0.9 reduce_sum.27
  47.3 10.4 %all_to_all.56 = f32[4,80,128]{2,1,0:T(8,128)S(1)} all-to-all(f32[4,80,128]{2,1,0:T(8,128)S(1)} %broadcast_in_dim.24), channel_id=1, replica_groups={{0,8,16,24},{32,40,48,56},{64,72,80,88},{96,104,112,120},{1,9,17,25},{3..., dimensions={0} | all-to-all | bytes 327680 | tf_op jit(solution)/shard_map/all_to_all | solution.py:259
  57.7 0.9 copy-done.3
  58.6 0.8 copy-done.5
  59.5 0.8 copy-done.7
  60.3 5.0 %shard_map.90 = (f32[320,128]{1,0:T(8,128)S(1)}, f32[512,128]{1,0:T(8,128)}) custom-call(f32[320,128]{1,0:T(8,128)S(1)} %bitcast.15, bf16[1280,192]{1,0:T(8,128)(2,1)S(1)} %get-tuple-element.35.parts_ref, bf16[512,1280]{1,0:T(8,128)(2,1)S(1)} %get-tuple-element.36.wide_ref, f32[128,128]{1,0:T(8,128)S(1)} %get-tuple-element.37.noise_ref, ...), custom_call_target="tpu_custom_call" | custom-call | flops 2147483648 | bytes 2097152 | tf_op jit(solution)/shard_map/pallas_call | solution.py:284
  65.3 6.0 %all-to-all-start.4 = ((f32[64,8,128]{2,1,0:T(8,128)}), f32[64,8,128]{2,1,0:T(8,128)S(1)}, u32[]{:S(2)}, u32[]{:S(2)}) async-start(f32[64,8,128]{2,1,0:T(8,128)} %bitcast.10), calls=%async_computation.4 | async-start | bytes 524288 | tf_op jit(solution)/shard_map/all_to_all | solution.py:251
  71.2 4.3 %collective-permute-start.2 = (f32[320,128]{1,0:T(8,128)S(1)}, f32[320,128]{1,0:T(8,128)S(1)}, u32[]{:S(2)}, u32[]{:S(2)}) collective-permute-start(f32[320,128]{1,0:T(8,128)S(1)} %get-tuple-element.42.refs_0_), channel_id=1, source_target_pairs={{0,384},{128,0},{256,128},{384,256},{1,385},{129,1},{257,129},{385... | collective-permute-start | bytes 491528 | tf_op jit(solution)/shard_map/ppermute | solution.py:341
  75.6 2.3 %collective-permute-start.1 = (f32[320,128]{1,0:T(8,128)S(1)}, f32[320,128]{1,0:T(8,128)S(1)}, u32[]{:S(2)}, u32[]{:S(2)}) collective-permute-start(f32[320,128]{1,0:T(8,128)S(1)} %get-tuple-element.42.refs_0_), channel_id=1, source_target_pairs={{0,256},{128,384},{256,0},{384,128},{1,257},{129,385},{257,1},{385... | collective-permute-start | bytes 491528 | tf_op jit(solution)/shard_map/ppermute | solution.py:341
  77.9 2.6 %collective-permute-start = (f32[320,128]{1,0:T(8,128)S(1)}, f32[320,128]{1,0:T(8,128)S(1)}, u32[]{:S(2)}, u32[]{:S(2)}) collective-permute-start(f32[320,128]{1,0:T(8,128)S(1)} %get-tuple-element.42.refs_0_), channel_id=1, source_target_pairs={{0,128},{128,256},{256,384},{384,0},{1,129},{129,257},{257,385},{3... | collective-permute-start | bytes 491528 | tf_op jit(solution)/shard_map/ppermute | solution.py:341
  80.5 6.3 %all-to-all-done.4 = f32[64,8,128]{2,1,0:T(8,128)S(1)} async-done(((f32[64,8,128]{2,1,0:T(8,128)}), f32[64,8,128]{2,1,0:T(8,128)S(1)}, u32[]{:S(2)}, u32[]{:S(2)}) %all-to-all-start.4) | async-done | bytes 262176 | tf_op jit(solution)/shard_map/all_to_all | solution.py:251
  86.7 0.1 reduce_sum.28
  86.8 0.0 collective-permute-done.2.refs_3_
  86.8 0.0 collective-permute-done.1.refs_2_
  86.8 0.0 collective-permute-done.refs_1_
  86.8 0.6 broadcast_in_dim.25
  87.5 11.5 %all-to-all-start.5 = ((f32[8,8,128]{2,1,0:T(8,128)}), f32[8,8,128]{2,1,0:T(8,128)S(1)}, u32[]{:S(2)}, u32[]{:S(2)}) async-start(f32[8,8,128]{2,1,0:T(8,128)} %broadcast_in_dim.25), calls=%async_computation.5 | async-start | bytes 65536 | tf_op jit(solution)/shard_map/all_to_all | solution.py:259
  98.9 1.6 %shard_map.91 = f32[1280,128]{1,0:T(8,128)} custom-call(f32[320,128]{1,0:T(8,128)S(1)} %get-tuple-element.42.refs_0_, f32[320,128]{1,0:T(8,128)S(1)} %collective-permute-done.refs_1_, f32[320,128]{1,0:T(8,128)S(1)} %collective-permute-done.1.refs_2_, f32[320,128]{1,0:T(8,128)S(1)} %collective-permute-done.2.refs_3_), custom_call_target="tpu_custom_call" | custom-call | tf_op jit(solution)/shard_map/pallas_call | solution.py:284
  100.5 3.1 %all-to-all-done.5 = f32[8,8,128]{2,1,0:T(8,128)S(1)} async-done(((f32[8,8,128]{2,1,0:T(8,128)}), f32[8,8,128]{2,1,0:T(8,128)S(1)}, u32[]{:S(2)}, u32[]{:S(2)}) %all-to-all-start.5) | async-done | bytes 32800 | tf_op jit(solution)/shard_map/all_to_all | solution.py:259
  103.6 0.6 reduce_sum.29
  (10 shorter events, 0.0 us)
Async XLA Ops:
  0.6 35.1 %copy-start.1 = (s32[512]{0:T(512)S(1)}, s32[512]{0:T(512)}, u32[]{:S(2)}) copy-start(s32[512]{0:T(512)} %param.13) | copy-start | bytes 6148
  0.6 35.1 %copy-start = (f32[20,64,64]{2,1,0:T(8,128)S(1)}, f32[20,64,64]{2,1,0:T(8,128)}, u32[]{:S(2)}) copy-start(f32[20,64,64]{2,1,0:T(8,128)} %mix_ref.1) | copy-start | bytes 983044
  25.3 21.0 %all-to-all-start.2 = ((f32[4,80,128]{2,1,0:T(8,128)}), f32[4,80,128]{2,1,0:T(8,128)}, u32[]{:S(2)}, u32[]{:S(2)}) async-start(f32[4,80,128]{2,1,0:T(8,128)} %bitcast.7), calls=%async_computation.2 | async-start | bytes 327680 | tf_op jit(solution)/shard_map/all_to_all | solution.py:251
  39.5 0.7 copy-start.2
  40.2 0.6 copy-start.4
  40.8 0.6 copy-start.6
  57.7 1.0 copy-start.3
  58.6 0.8 copy-start.5
  59.5 0.8 copy-start.7
  65.3 21.5 %all-to-all-start.4 = ((f32[64,8,128]{2,1,0:T(8,128)}), f32[64,8,128]{2,1,0:T(8,128)S(1)}, u32[]{:S(2)}, u32[]{:S(2)}) async-start(f32[64,8,128]{2,1,0:T(8,128)} %bitcast.10), calls=%async_computation.4 | async-start | bytes 524288 | tf_op jit(solution)/shard_map/all_to_all | solution.py:251
  71.2 15.6 %collective-permute-start.2 = (f32[320,128]{1,0:T(8,128)S(1)}, f32[320,128]{1,0:T(8,128)S(1)}, u32[]{:S(2)}, u32[]{:S(2)}) collective-permute-start(f32[320,128]{1,0:T(8,128)S(1)} %get-tuple-element.42.refs_0_), channel_id=1, source_target_pairs={{0,384},{128,0},{256,128},{384,256},{1,385},{129,1},{257,129},{385... | collective-permute-start | bytes 491528 | tf_op jit(solution)/shard_map/ppermute | solution.py:341
  75.6 11.2 %collective-permute-start.1 = (f32[320,128]{1,0:T(8,128)S(1)}, f32[320,128]{1,0:T(8,128)S(1)}, u32[]{:S(2)}, u32[]{:S(2)}) collective-permute-start(f32[320,128]{1,0:T(8,128)S(1)} %get-tuple-element.42.refs_0_), channel_id=1, source_target_pairs={{0,256},{128,384},{256,0},{384,128},{1,257},{129,385},{257,1},{385... | collective-permute-start | bytes 491528 | tf_op jit(solution)/shard_map/ppermute | solution.py:341
  77.9 9.0 %collective-permute-start = (f32[320,128]{1,0:T(8,128)S(1)}, f32[320,128]{1,0:T(8,128)S(1)}, u32[]{:S(2)}, u32[]{:S(2)}) collective-permute-start(f32[320,128]{1,0:T(8,128)S(1)} %get-tuple-element.42.refs_0_), channel_id=1, source_target_pairs={{0,128},{128,256},{256,384},{384,0},{1,129},{129,257},{257,385},{3... | collective-permute-start | bytes 491528 | tf_op jit(solution)/shard_map/ppermute | solution.py:341
  87.5 16.2 %all-to-all-start.5 = ((f32[8,8,128]{2,1,0:T(8,128)}), f32[8,8,128]{2,1,0:T(8,128)S(1)}, u32[]{:S(2)}, u32[]{:S(2)}) async-start(f32[8,8,128]{2,1,0:T(8,128)} %broadcast_in_dim.25), calls=%async_computation.5 | async-start | bytes 65536 | tf_op jit(solution)/shard_map/all_to_all | solution.py:259
